TPU v7x, 256 devices: a whole 4x4x8 slice. The times are simulated.
256 devices in a mesh: space: 64 (over z, x, core), tm: 4 (over y).
Axes of the slice: x: 4, y: 4, z: 8, core: 2. Of those that a mesh axis runs over, the one named last changes fastest.
Arguments:
- terminal: float32 [4, 64, 64, 8, 128], P('tm', None, 'space'), may hold values from -6 to 6
- goal_weight: float32 [64, 64, 8, 128], P(None, 'space'), may hold values from -4 to 4
- conduct: float32 [64, 8, 128], P('space'), may hold values from 0.02 to 0.16
- active_count: int32 [4], P('tm'), may hold values from 4 to 8
Outputs:
- basis: float32 [256, 65536], P('tm', 'space')
Inputs may be any that keep to these rules, and one draw needn't show every extreme that they name: `active_count`: active layers count from the bottom of the embankment.
All inputs are finite; a program needn't handle non-finite values.
Results may differ from a plain program's by a relative error of at most 0.0001.
Values sent between devices are 32-bit elements; how exact they have to be, the bound alone decides.
A program may use at most 64 MiB of HBM per device.

v0:
```python
import jax
import jax.numpy as jnp
from jax import lax
from jax.sharding import PartitionSpec as P

STEPS = 4
LAYERS = 8
SIGN_STEPS = 2


def with_halo(shard, sides, width):
    for axis, dim in sides:
        devices, length = (lax.axis_size(axis), shard.shape[dim])
        up = [(i, (i + 1) % devices) for i in range(devices - 1)]
        down = [(j, i) for i, j in up]
        last = lax.slice_in_dim(shard, length - width, length, axis=dim)
        leading = lax.slice_in_dim(shard, 0, width, axis=dim)
        before = lax.ppermute(last, axis, up)
        after = lax.ppermute(leading, axis, down)
        shard = jnp.concatenate([before, shard, after], axis=dim)
    return shard


def from_behind(value, axis, steps):
    count = lax.axis_size(axis)
    leading, last = (max(0, -steps), min(count, count - steps))
    return lax.ppermute(value, axis, [(source, source + steps) for source in range(leading, last)])


def broadcast(value, axis, source):
    kept = jnp.where(lax.axis_index(axis) == source, value, 0).astype(value.dtype)
    return lax.psum(kept, axis)


def product(left, right):
    return jnp.dot(left, right, precision=lax.Precision.HIGHEST)


def outer_gram(rows):
    return lax.dot_general(rows, rows, (((1,), (1,)), ((), ())), precision=lax.Precision.HIGHEST)


def filter_weights(gram_matrix):
    order_size = gram_matrix.shape[0]
    half_size = order_size // 2
    identity = jnp.eye(order_size, dtype=jnp.float32)
    energy = jnp.trace(gram_matrix) / order_size + 1e-06
    shifted = gram_matrix / energy - identity
    sign_iter = shifted / jnp.sqrt(jnp.sum(shifted * shifted) + 1e-06)
    for repeat in range(SIGN_STEPS):
        sign_iter = 0.5 * product(sign_iter, 3.0 * identity - product(sign_iter, sign_iter))
    keep_part = 0.5 * (identity + sign_iter)
    weights = (keep_part[:, :half_size] + keep_part[:, half_size:]) * (
        1.0 / jnp.sqrt(jnp.float32(2.0))
    )
    kept_energy = jnp.sum(weights * product(gram_matrix, weights))
    return weights * jnp.sqrt(energy * half_size / (kept_energy + 1e-06))


def merge_pair(lower_panel, upper_panel):
    stacked = jnp.concatenate([lower_panel, upper_panel], 0)
    gram_matrix = lax.psum(outer_gram(stacked), "space")
    weights = filter_weights(gram_matrix)
    return lax.dot_general(
        weights, stacked, (((0,), (0,)), ((), ())), precision=lax.Precision.HIGHEST
    )


def neighbours(padded):
    total = padded[:, 2:, 1:-1, 1:-1] + padded[:, :-2, 1:-1, 1:-1]
    total = total + padded[:, 1:-1, 2:, 1:-1] + padded[:, 1:-1, :-2, 1:-1]
    total = total + padded[:, 1:-1, 1:-1, 2:] + padded[:, 1:-1, 1:-1, :-2]
    return total


def shards(terminal, goal_weight, conduct, active_count):
    adjoint_field = terminal[0]
    depth = adjoint_field.shape[3]
    layer_index = jnp.arange(depth) // (depth // LAYERS)
    active_mask = (layer_index < active_count[0]).astype(jnp.float32)
    adjoint_field = adjoint_field * active_mask
    snapshots = []
    for repeat in range(STEPS):
        extended = with_halo(adjoint_field, (("space", 1),), 1)
        padded = jnp.pad(extended, ((0, 0), (0, 0), (1, 1), (1, 1)))
        adjoint_field = active_mask * (
            adjoint_field + conduct * (neighbours(padded) - 6.0 * adjoint_field) + goal_weight
        )
        snapshots.append(adjoint_field.reshape(adjoint_field.shape[0], -1))
    panel = jnp.concatenate(snapshots, 0)
    levels_count = lax.axis_size("tm").bit_length() - 1
    position = lax.axis_index("tm")
    for merge_level in range(levels_count):
        lower_panel = panel
        upper_panel = from_behind(panel, "tm", -(1 << merge_level))
        panel = merge_pair(lower_panel, upper_panel)
    panel = broadcast(panel, "tm", 0)
    rows_each = panel.shape[0] // lax.axis_size("tm")
    return lax.dynamic_slice_in_dim(panel, position * rows_each, rows_each, 0)


def solution(mesh):
    placed = (
        P("tm", None, "space", None, None),
        P(None, "space", None, None),
        P("space", None, None),
        P("tm"),
    )
    return jax.shard_map(
        shards, mesh=mesh, in_specs=placed, out_specs=P("tm", "space"), check_vma=False
    )
```

profile of v0, /device:TPU:1, one launch (start us, length us, event | category | flops | bytes accessed | tf_op | source)
XLA Modules:
  0.0 587.6 jit_solution(5532125705987556607)
XLA Ops:
  7.3 1.0 bitcast_multiply_fusion
  8.2 5.1 collective-permute-start
  13.4 1.9 collective-permute-start.1
  15.3 1.5 collective-permute-done
  16.8 1.8 collective-permute-done.1
  18.6 0.9 select_maximum_fusion.6
  19.5 0.3 fusion.34
  19.8 1.9 collective-permute-start.2
  21.8 4.4 collective-permute-start.3
  26.2 2.1 collective-permute-done.2
  28.3 1.2 collective-permute-done.3
  29.5 0.9 select_maximum_fusion.4
  30.7 1.9 collective-permute-start.4
  32.6 4.4 collective-permute-start.5
  37.0 2.1 collective-permute-done.4
  39.1 1.2 collective-permute-done.5
  40.3 0.9 select_maximum_fusion.2
  41.5 1.9 collective-permute-start.6
  43.4 4.4 collective-permute-start.7
  48.0 1.9 collective-permute-done.6
  49.9 1.2 collective-permute-done.7
  51.1 0.9 select_maximum_fusion
  52.4 1.3 collective-permute-start.8
  53.9 21.6 %collective-permute-done.8 = f32[256,1024]{1,0:T(8,128)S(1)} collective-permute-done((f32[256,1024]{1,0:T(8,128)S(1)}, f32[256,1024]{1,0:T(8,128)S(1)}, u32[]{:S(2)}, u32[]{:S(2)}) %collective-permute-start.8) | collective-permute-done | bytes 1048608 | tf_op jit(solution)/shard_map/ppermute | solution.py:27
  75.6 4.6 fusion.43
  80.4 197.7 %all-reduce.8.cloned.1.call-done = f32[512,512]{1,0:T(8,128)} async-done(((f32[512,512]{1,0:T(8,128)}), f32[512,512]{1,0:T(8,128)}) %all-reduce.8.cloned.1.call-update) | async-done | bytes 1048592 | tf_op jit(solution)/shard_map/psum | solution.py:62
  278.2 1.9 select_reduce_fusion.1
  280.7 2.1 multiply_reduce_fusion.1
  283.5 3.6 select_subtract_fusion.3
  287.2 1.9 convolution_multiply_fusion.3
  289.1 1.8 select_subtract_fusion.2
  291.0 1.8 fusion.6
  292.8 1.6 fusion.8
  295.2 1.9 fusion.12
  297.1 1.5 collective-permute-start.9
  298.6 24.3 %collective-permute-done.9 = f32[256,1024]{1,0:T(8,128)S(1)} collective-permute-done((f32[256,1024]{1,0:T(8,128)S(1)}, f32[256,1024]{1,0:T(8,128)S(1)}, u32[]{:S(2)}, u32[]{:S(2)}) %collective-permute-start.9) | collective-permute-done | bytes 1048608 | tf_op jit(solution)/shard_map/ppermute | solution.py:27
  322.9 4.5 fusion.4
  327.5 182.9 %all-reduce.10.cloned.1.call-done = f32[512,512]{1,0:T(8,128)} async-done(((f32[512,512]{1,0:T(8,128)}), f32[512,512]{1,0:T(8,128)}) %all-reduce.10.cloned.1.call-update) | async-done | bytes 1048592 | tf_op jit(solution)/shard_map/psum | solution.py:62
  510.4 1.9 select_reduce_fusion
  512.9 2.1 multiply_reduce_fusion
  515.7 3.8 select_subtract_fusion.1
  519.5 1.9 convolution_multiply_fusion.1
  521.5 1.8 select_subtract_fusion
  523.3 1.8 fusion.7
  525.2 1.6 fusion.9
  527.5 2.9 fusion.5
  530.5 48.9 %all-reduce.12.cloned.1.call-done = f32[256,1024]{1,0:T(8,128)} async-done(((f32[256,1024]{1,0:T(8,128)}), f32[256,1024]{1,0:T(8,128)}) %all-reduce.12.cloned.1.call-update) | async-done | bytes 1048592 | tf_op jit(solution)/shard_map/psum | solution.py:32
  579.4 1.7 constant_dynamic-slice_fusion
  (34 shorter events, 1.8 us)
Async XLA Ops:
  6.5 13.0 %copy-start.5 = (f32[1,64,1,8,128]{4,3,2,1,0:T(8,128)S(1)}, f32[1,64,1,8,128]{4,3,2,1,0:T(8,128)}, u32[]{:S(2)}) copy-start(f32[1,64,1,8,128]{4,3,2,1,0:T(8,128)} %param.4) | copy-start | bytes 786436
  6.5 13.0 %copy-start.6 = (f32[1,8,128]{2,1,0:T(8,128)S(1)}, f32[1,8,128]{2,1,0:T(8,128)}, u32[]{:S(2)}) copy-start(f32[1,8,128]{2,1,0:T(8,128)} %param.6) | copy-start | bytes 12292
  6.5 13.0 %copy-start.4 = (f32[64,1,8,128]{3,2,1,0:T(8,128)S(1)}, f32[64,1,8,128]{3,2,1,0:T(8,128)}, u32[]{:S(2)}) copy-start(f32[64,1,8,128]{3,2,1,0:T(8,128)} %param.5) | copy-start | bytes 786436
  6.5 271.6 %all-reduce.8.cloned.1.call-start = ((), (), s32[]{:S(2)}) async-start(), calls=%async_computation | async-start | bytes 2097152 | tf_op jit(solution)/shard_map/psum | solution.py:62
  8.2 8.6 %collective-permute-start = (f32[64,1,8,128]{3,2,1,0:T(8,128)S(1)}, f32[64,1,8,128]{3,2,1,0:T(8,128)S(1)}, u32[]{:S(2)}, u32[]{:S(2)}) collective-permute-start(f32[64,1,8,128]{3,2,1,0:T(8,128)S(1)} %bitcast_multiply_fusion), channel_id=1, source_target_pairs={{4,0},{8,4},{12,8},{16,12},{20,16},{24,20},{28,24},{32,28},{36,32}... | collective-permute-start | bytes 786440 | tf_op jit(solution)/shard_map/ppermute | solution.py:19
  13.4 5.2 collective-permute-start.1
  19.8 8.4 %collective-permute-start.2 = (f32[64,1,8,128]{3,2,1,0:T(8,128)S(1)}, f32[64,1,8,128]{3,2,1,0:T(8,128)S(1)}, u32[]{:S(2)}, u32[]{:S(2)}) collective-permute-start(f32[64,1,8,128]{3,2,1,0:T(8,128)S(1)} %fusion.34), channel_id=1, source_target_pairs={{4,0},{8,4},{12,8},{16,12},{20,16},{24,20},{28,24},{32,28},{36,32}... | collective-permute-start | bytes 786440 | tf_op jit(solution)/shard_map/ppermute | solution.py:19
  21.8 7.7 %collective-permute-start.3 = (f32[64,1,8,128]{3,2,1,0:T(8,128)S(1)}, f32[64,1,8,128]{3,2,1,0:T(8,128)S(1)}, u32[]{:S(2)}, u32[]{:S(2)}) collective-permute-start(f32[64,1,8,128]{3,2,1,0:T(8,128)S(1)} %fusion.34), channel_id=1, source_target_pairs={{0,4},{4,8},{8,12},{12,16},{16,20},{20,24},{24,28},{28,32},{32,36}... | collective-permute-start | bytes 786440 | tf_op jit(solution)/shard_map/ppermute | solution.py:18
  30.7 8.4 %collective-permute-start.4 = (f32[64,1,8,128]{3,2,1,0:T(8,128)S(1)}, f32[64,1,8,128]{3,2,1,0:T(8,128)S(1)}, u32[]{:S(2)}, u32[]{:S(2)}) collective-permute-start(f32[64,1,8,128]{3,2,1,0:T(8,128)S(1)} %fusion.29), channel_id=1, source_target_pairs={{4,0},{8,4},{12,8},{16,12},{20,16},{24,20},{28,24},{32,28},{36,32}... | collective-permute-start | bytes 786440 | tf_op jit(solution)/shard_map/ppermute | solution.py:19
  32.6 7.7 %collective-permute-start.5 = (f32[64,1,8,128]{3,2,1,0:T(8,128)S(1)}, f32[64,1,8,128]{3,2,1,0:T(8,128)S(1)}, u32[]{:S(2)}, u32[]{:S(2)}) collective-permute-start(f32[64,1,8,128]{3,2,1,0:T(8,128)S(1)} %fusion.29), channel_id=1, source_target_pairs={{0,4},{4,8},{8,12},{12,16},{16,20},{20,24},{24,28},{28,32},{32,36}... | collective-permute-start | bytes 786440 | tf_op jit(solution)/shard_map/ppermute | solution.py:18
  41.5 8.4 %collective-permute-start.6 = (f32[64,1,8,128]{3,2,1,0:T(8,128)S(1)}, f32[64,1,8,128]{3,2,1,0:T(8,128)S(1)}, u32[]{:S(2)}, u32[]{:S(2)}) collective-permute-start(f32[64,1,8,128]{3,2,1,0:T(8,128)S(1)} %fusion.24), channel_id=1, source_target_pairs={{4,0},{8,4},{12,8},{16,12},{20,16},{24,20},{28,24},{32,28},{36,32}... | collective-permute-start | bytes 786440 | tf_op jit(solution)/shard_map/ppermute | solution.py:19
  43.4 7.7 %collective-permute-start.7 = (f32[64,1,8,128]{3,2,1,0:T(8,128)S(1)}, f32[64,1,8,128]{3,2,1,0:T(8,128)S(1)}, u32[]{:S(2)}, u32[]{:S(2)}) collective-permute-start(f32[64,1,8,128]{3,2,1,0:T(8,128)S(1)} %fusion.24), channel_id=1, source_target_pairs={{0,4},{4,8},{8,12},{12,16},{16,20},{20,24},{24,28},{28,32},{32,36}... | collective-permute-start | bytes 786440 | tf_op jit(solution)/shard_map/ppermute | solution.py:18
  52.4 23.1 %collective-permute-start.8 = (f32[256,1024]{1,0:T(8,128)S(1)}, f32[256,1024]{1,0:T(8,128)S(1)}, u32[]{:S(2)}, u32[]{:S(2)}) collective-permute-start(f32[256,1024]{1,0:T(8,128)S(1)} %pad_maximum_fusion.5), channel_id=1, source_target_pairs={{1,0},{2,1},{3,2},{5,4},{6,5},{7,6},{9,8},{10,9},{11,10},{13,12},{... | collective-permute-start | bytes 3145736 | tf_op jit(solution)/shard_map/ppermute | solution.py:27
  80.2 430.2 %all-reduce.10.cloned.1.call-start = ((), (), s32[]{:S(2)}) async-start(), calls=%async_computation.1 | async-start | bytes 2097152 | tf_op jit(solution)/shard_map/psum | solution.py:62
  283.5 3.7 copy-start.1
  297.1 25.8 %copy-start.2 = (f32[256,1024]{1,0:T(8,128)}, f32[256,1024]{1,0:T(8,128)S(1)}, u32[]{:S(2)}) copy-start(f32[256,1024]{1,0:T(8,128)S(1)} %fusion.12) | copy-start | bytes 3145732
  297.1 25.8 %collective-permute-start.9 = (f32[256,1024]{1,0:T(8,128)S(1)}, f32[256,1024]{1,0:T(8,128)S(1)}, u32[]{:S(2)}, u32[]{:S(2)}) collective-permute-start(f32[256,1024]{1,0:T(8,128)S(1)} %fusion.12), channel_id=1, source_target_pairs={{2,0},{3,1},{6,4},{7,5},{10,8},{11,9},{14,12},{15,13},{18,16},{19,... | collective-permute-start | bytes 3145736 | tf_op jit(solution)/shard_map/ppermute | solution.py:27
  327.4 252.0 %all-reduce.12.cloned.1.call-start = ((), (), s32[]{:S(2)}) async-start(), calls=%async_computation.2 | async-start | bytes 2097152 | tf_op jit(solution)/shard_map/psum | solution.py:32
  515.7 3.8 copy-start
  523.3 4.2 copy-start.3
Sparse Core Ops, SparseCore 0:
  80.3 197.8 all-reduce.7
  327.5 182.7 all-reduce.9
  530.6 48.7 all-reduce.11
where the time goes:
time: 589 us; the launch traced here: 588 us
  waiting for transfers between devices  488 us (83%)
  matrix products  35.8 us (6%)
  starting transfers between devices  29.1 us (5%)
  between operations  18.4 us (3%)
  other arithmetic  13.8 us (2%)
    psum x2, waiting for transfers between devices, merge_pair(): gram_matrix = lax.psum(outer_gram(stacked), 'space')  381 us
    psum x1, waiting for transfers between devices, broadcast(): return lax.psum(kept, axis)  48.9 us
    ppermute x2, waiting for transfers between devices, from_behind(): lax.ppermute(value, axis, [(source, source + steps) for source in range(l...  45.9 us
    dot_general x10, matrix products, product(): return jnp.dot(left, right, precision=lax.Precision.HIGHEST)  21.9 us
    ppermute x4, starting transfers between devices, with_halo(): before = lax.ppermute(last, axis, up)  15.1 us
  transfers between devices with their start and end apart: 13, of which 13 were waited for; matrix products, arithmetic and copies ran while one was open for 0% of the time, Pallas kernels for 0%

commit v1 on v0

v1 whole, which is shorter than its diff:
```python
import jax
import jax.numpy as jnp
from jax import lax
from jax.experimental import pallas as pl
from jax.experimental.pallas import tpu as pltpu
from jax.sharding import PartitionSpec as P

STEPS = 4
GOALS = 64
LAYERS = 8
NX_CHIPS = 4
N_TM = 4
CHUNKS = 2
F32 = jnp.float32
BF16 = jnp.bfloat16


def split(x):
    high = x.astype(BF16)
    return high, (x - high.astype(F32)).astype(BF16)


def dot(a, b, dims):
    return lax.dot_general(a, b, (dims, ((), ())), preferred_element_type=F32)


def dot3(ah, al, bh, bl, dims=((1,), (0,))):
    return dot(ah, bh, dims) + (dot(ah, bl, dims) + dot(al, bh, dims))


NT = ((1,), (1,))


class Links:
    def __init__(self, send_sems, recv_sems):
        self.send_sems, self.recv_sems, self.copies = send_sems, recv_sems, []

    def start(self, src, dst, device):
        n = len(self.copies)
        copy = pltpu.make_async_remote_copy(
            src_ref=src, dst_ref=dst, send_sem=self.send_sems.at[n], recv_sem=self.recv_sems.at[n],
            device_id=device, device_id_type=pl.DeviceIdType.MESH)
        copy.start()
        self.copies.append(copy)
        return copy

    def finish(self):
        for copy in self.copies:
            copy.wait_send()


def rows(start, size):
    return pl.ds(pl.multiple_of(start, 8), size)


def kernel(n_space, term_ref, goal_ref, cond_ref, count_ref, out_ref,
           field, goal, halo_l, halo_r, own, other, sh, sl,
           pg, pc, rx1, ry1, qx1, qy1, rx2, ry2, qz, rz, fz, q2x, q2y, gf,
           cx1, cy1, dx1, dy1, cx2, cy2, ez, crz, cfz, d2x, d2y, cb,
           gmat, s0f, s0h, s0l, zh, zl, s1h, s1l, ff, fh, fl, th, tl, wf, wh, wl, wt,
           wb, hb, mh, ml, g2, bs, send_sems, recv_sems):
    s = lax.axis_index("space")
    t = lax.axis_index("tm")
    core = s % 2
    chip = s // 2
    cx = chip % NX_CHIPS
    cz = chip // NX_CHIPS
    n_z = n_space // (2 * NX_CHIPS)
    left = (lax.rem(s + n_space - 1, n_space), t)
    right = (lax.rem(s + 1, n_space), t)
    partner = (s + 1 - 2 * core, t)

    def y_peer(d):
        return lax.rem(t + d, N_TM)

    def x_peer(d):
        return lax.rem(cx + d, NX_CHIPS)

    def z_peer(d):
        return lax.rem(cz + d, n_z)

    def at_y(d):
        return (s, y_peer(d))

    def at_x(d):
        return ((cz * NX_CHIPS + x_peer(d)) * 2 + core, t)

    def at_z(d):
        return ((z_peer(d) * NX_CHIPS + cx) * 2 + core, t)

    peers = [left, right] + [at_y(d) for d in range(1, N_TM)] + [at_x(d) for d in range(1, NX_CHIPS)]
    peers += [at_z(d) for d in range(1, n_z)]
    barrier = pltpu.get_barrier_semaphore()
    for peer in peers:
        pl.semaphore_signal(barrier, inc=1, device_id=peer, device_id_type=pl.DeviceIdType.MESH)

    lane = lax.broadcasted_iota(jnp.int32, (1, 128), 1)
    mask = (lane // (128 // LAYERS) < count_ref[0]).astype(F32)
    for y in range(8):
        field[0, y] = term_ref[pl.ds(y, GOALS, stride=8), :] * mask
        goal[y] = goal_ref[pl.ds(y, GOALS, stride=8), :] * mask
    pl.semaphore_wait(barrier, len(peers))

    links = Links(send_sems, recv_sems)
    size = GOALS // CHUNKS

    def part(c):
        return pl.ds(c * size, size)

    def send_halo(k, c):
        to_right = links.start(field.at[k, :, part(c)], halo_l.at[k, :, part(c)], right)
        to_left = links.start(field.at[k, :, part(c)], halo_r.at[k, :, part(c)], left)
        return to_right, to_left

    has_left = jnp.where(s > 0, 1.0, 0.0).astype(F32)
    has_right = jnp.where(s < n_space - 1, 1.0, 0.0).astype(F32)
    inner_lo = (lane > 0).astype(F32)
    inner_hi = (lane < 127).astype(F32)
    halos = {(0, c): send_halo(0, c) for c in range(CHUNKS)}
    spread = {}

    def absorb(k):
        for ref, base in ((own, 0), (other, 256)):
            for yy in range(2):
                for b in range(N_TM):
                    high, low = split(ref[k, yy, pl.ds(b * GOALS, GOALS), :])
                    sh[b, pl.ds(k * GOALS, GOALS), pl.ds(base + yy * 128, 128)] = high
                    sl[b, pl.ds(k * GOALS, GOALS), pl.ds(base + yy * 128, 128)] = low

    shared = {}
    for k in range(STEPS):
        for c in range(CHUNKS):
            for copy in halos[k, c]:
                copy.wait_recv()
            for y in range(8):
                here = field[k, y, part(c)]
                total = halo_l[k, y, part(c)] * has_left + halo_r[k, y, part(c)] * has_right
                if y > 0:
                    total = total + field[k, y - 1, part(c)]
                if y < 7:
                    total = total + field[k, y + 1, part(c)]
                total = total + pltpu.roll(here, 1, 1) * inner_lo + pltpu.roll(here, 127, 1) * inner_hi
                kappa = cond_ref[pl.ds(y, 1), :]
                field[k + 1, y, part(c)] = mask * (
                    here + kappa * (total - 6.0 * here)) + goal[y, part(c)]
            if k + 1 < STEPS:
                halos[k + 1, c] = send_halo(k + 1, c)
            spread[k, c] = [
                links.start(field.at[k + 1, pl.ds(2 * y_peer(d), 2), part(c)],
                            own.at[k, :, rows(t * GOALS + c * size, size)], at_y(d))
                for d in range(1, N_TM)]
            own[k, :, rows(t * GOALS + c * size, size)] = field[k + 1, pl.ds(2 * t, 2), part(c)]
        if k > 0:
            shared[k - 1] = share(links, spread, own, other, k - 1, partner)
    shared[STEPS - 1] = share(links, spread, own, other, STEPS - 1, partner)
    for k in range(STEPS):
        shared[k].wait_recv()
        absorb(k)

    lower, upper = 2 * core, 2 * core + 1

    def gram(i, j):
        return dot3(sh[i], sl[i], sh[j], sl[j], NT)

    for n, (i, j) in enumerate(((lower, lower), (lower, upper), (upper, upper))):
        g = gram(i, j)
        pg[pl.ds(n * 512, 256)] = g[:, :128]
        pg[pl.ds(n * 512 + 256, 256)] = g[:, 128:]
    for n, j in enumerate((2, 3)):
        g = gram(core, j)
        pc[pl.ds(n * 512, 256)] = g[:, :128]
        pc[pl.ds(n * 512 + 256, 256)] = g[:, 128:]

    def scatter(src, base, land, length, peer, at, count):
        return [links.start(src.at[rows(base + peer(d) * length, length)], land.at[d - 1], at(d))
                for d in range(1, count)]

    def reduced(src, base, land, length, copies, place):
        total = src[rows(base + place * length, length)]
        for d, copy in enumerate(copies):
            copy.wait_recv()
            total = total + land[d]
        return total

    def gather(src, dst, base, length, place, at, count):
        return [links.start(src, dst.at[rows(base + place * length, length)], at(d)) for d in range(1, count)]

    def wait(copies):
        for copy in copies:
            copy.wait_recv()

    def stage1(src, landx, landy):
        half = src.shape[0] // 2
        return (scatter(src, 0, landx, half // 4, x_peer, at_x, NX_CHIPS),
                scatter(src, half, landy, half // 4, y_peer, at_y, N_TM))

    def stage2(src, landx, landy, copies, qx, qy, landx2, landy2):
        half = src.shape[0] // 2
        qx[...] = reduced(src, 0, landx, half // 4, copies[0], cx)
        first = scatter(qx, 0, landx2, half // 16, y_peer, at_y, N_TM)
        qy[...] = reduced(src, half, landy, half // 4, copies[1], t)
        return first, scatter(qy, 0, landy2, half // 16, x_peer, at_x, NX_CHIPS)

    def stage3(qx, qy, landx2, landy2, copies, q, land):
        length = qx.shape[0] // 4
        q[pl.ds(0, length)] = reduced(qx, 0, landx2, length, copies[0], t)
        q[pl.ds(length, length)] = reduced(qy, 0, landy2, length, copies[1], cx)
        if q.shape[0] > 2 * length:
            q[pl.ds(2 * length, q.shape[0] - 2 * length)] = jnp.zeros((q.shape[0] - 2 * length, 128), F32)
        return scatter(q, 0, land, q.shape[0] // n_z, z_peer, at_z, n_z)

    def back1(q, land, copies, full):
        length = q.shape[0] // n_z
        full[rows(cz * length, length)] = reduced(q, 0, land, length, copies, cz)
        return gather(full.at[rows(cz * length, length)], full, 0, length, cz, at_z, n_z)

    def back2(full, copies, qx, qy):
        wait(copies)
        length = qx.shape[0] // 4
        first = gather(full.at[pl.ds(0, length)], qx, 0, length, t, at_y, N_TM)
        second = gather(full.at[pl.ds(length, length)], qy, 0, length, cx, at_x, NX_CHIPS)
        qx[rows(t * length, length)] = full[pl.ds(0, length)]
        qy[rows(cx * length, length)] = full[pl.ds(length, length)]
        return first, second

    def back3(qx, qy, copies, dst):
        length = qx.shape[0]
        wait(copies[0])
        first = gather(qx, dst, 0, length, cx, at_x, NX_CHIPS)
        wait(copies[1])
        second = gather(qy, dst, 4 * length, length, t, at_y, N_TM)
        dst[rows(cx * length, length)] = qx[...]
        dst[rows(4 * length + t * length, length)] = qy[...]
        return first + second

    g1 = stage1(pg, rx1, ry1)
    g2c = stage2(pg, rx1, ry1, g1, qx1, qy1, rx2, ry2)
    c1 = stage1(pc, cx1, cy1)
    g3 = stage3(qx1, qy1, rx2, ry2, g2c, qz, rz)
    c2 = stage2(pc, cx1, cy1, c1, dx1, dy1, cx2, cy2)
    g4 = back1(qz, rz, g3, fz)
    g5 = back2(fz, g4, q2x, q2y)
    c3 = stage3(dx1, dy1, cx2, cy2, c2, ez, crz)
    g6 = back3(q2x, q2y, g5, gf)
    c4 = back1(ez, crz, c3, cfz)
    wait(g6)

    cmat = cb.at[core]

    def eye(size):
        return (lax.broadcasted_iota(jnp.int32, (size, size), 0)
                == lax.broadcasted_iota(jnp.int32, (size, size), 1)).astype(F32)

    def block(ref, n):
        return jnp.concatenate([ref[pl.ds(n * 512, 256)], ref[pl.ds(n * 512 + 256, 256)]], 1)

    upper_right = block(gf, 1)
    gmat[pl.ds(0, 256), pl.ds(0, 256)] = block(gf, 0)
    gmat[pl.ds(0, 256), pl.ds(256, 256)] = upper_right
    gmat[pl.ds(256, 256), pl.ds(0, 256)] = upper_right.T
    gmat[pl.ds(256, 256), pl.ds(256, 256)] = block(gf, 2)

    def weights(between):
        identity = eye(256)
        trace = jnp.sum(gmat[pl.ds(0, 256), pl.ds(0, 256)] * identity) + jnp.sum(
            gmat[pl.ds(256, 256), pl.ds(256, 256)] * identity)
        energy = trace / 512.0 + 1e-6
        inverse = 1.0 / energy
        norm2 = jnp.float32(0.0)
        for i in range(2):
            for j in range(2):
                part_ = gmat[pl.ds(256 * i, 256), pl.ds(256 * j, 256)] * inverse
                if i == j:
                    part_ = part_ - identity
                s0f[pl.ds(256 * i, 256), pl.ds(256 * j, 256)] = part_
                norm2 = norm2 + jnp.sum(part_ * part_)
        norm = jnp.sqrt(norm2 + 1e-6)
        scale = 1.0 / norm
        for i in range(2):
            r = pl.ds(256 * i, 256)
            value = s0f[r] * scale
            s0f[r] = value
            s0h[r], s0l[r] = split(value)
        between(0)
        for i in range(2):
            r = pl.ds(256 * i, 256)
            zh[r], zl[r] = split(dot3(s0h[r], s0l[r], s0h[...], s0l[...]))
        between(1)
        for i in range(2):
            r = pl.ds(256 * i, 256)
            s1 = 1.5 * s0f[r] - 0.5 * dot3(s0h[r], s0l[r], zh[...], zl[...])
            s1h[r], s1l[r] = split(s1)
            f = s1[:, :256] + s1[:, 256:]
            ff[r] = f
            fh[r], fl[r] = split(f)
        between(2)
        for i in range(2):
            r = pl.ds(256 * i, 256)
            th[r], tl[r] = split(dot3(s1h[r], s1l[r], fh[...], fl[...]))
        for i in range(2):
            r = pl.ds(256 * i, 256)
            u = dot3(s1h[r], s1l[r], th[...], tl[...])
            w = (identity + 1.5 * ff[r] - 0.5 * u) * (0.5 / 2.0 ** 0.5)
            wf[r] = w
            wh[r], wl[r] = split(w)
        between(3)
        kept = jnp.float32(0.0)
        for i in range(2):
            r = pl.ds(256 * i, 256)
            gw = wf[r] + norm * dot3(s0h[r], s0l[r], wh[...], wl[...])
            ff[r] = gw
            kept = kept + jnp.sum(wf[r] * gw)
        ratio = 256.0 * energy / (energy * kept + 1e-6)
        alpha = jnp.sqrt(energy * ratio / energy)
        return energy, alpha

    state = {}

    def between(n):
        if n == 0:
            state["c5"] = back2(cfz, c4, d2x, d2y)
        if n == 1:
            state["c6"] = back3(d2x, d2y, state["c5"], cmat)
        if n == 2:
            wait(state["c6"])
            state["c7"] = links.start(cmat, cmat, partner)

    energy, alpha = weights(between)
    for i in range(2):
        wf[pl.ds(256 * i, 256)] = wf[pl.ds(256 * i, 256)] * alpha
    wb[core] = wf[...]
    send_w = links.start(wb.at[core], wb.at[core], partner)
    for i in range(2):
        fh[pl.ds(256 * i, 256)], fl[pl.ds(256 * i, 256)] = split(ff[pl.ds(256 * i, 256)])
    wt[...] = wf[...].T
    ah, al = split(wt[...])
    hb[core] = (energy * alpha) * dot3(ah, al, fh[...], fl[...])
    send_h = links.start(hb.at[core], hb.at[core], partner)
    state["c7"].wait_recv()
    send_w.wait_recv()

    w1h, w1l = split(wb[1])
    th[...] = w1h
    tl[...] = w1l
    for i in range(2):
        r = pl.ds(256 * i, 256)
        ch, cl = split(jnp.concatenate([cb[i, pl.ds(256 * j, 256)] for j in range(4)], 1))
        fh[r], fl[r] = split(dot3(ch, cl, th[...], tl[...]))
    for p in range(2):
        ah, al = split(wb[p].T)
        if p == 0:
            cross = dot3(ah, al, fh[...], fl[...])
            gmat[pl.ds(0, 256), pl.ds(256, 256)] = cross
            gmat[pl.ds(256, 256), pl.ds(0, 256)] = cross.T
        for i in range(2):
            block_h = sh[2 * p + i, :, pl.ds(0, 256)]
            block_l = sl[2 * p + i, :, pl.ds(0, 256)]
            term = dot3(ah[:, 256 * i:256 * i + 256], al[:, 256 * i:256 * i + 256], block_h, block_l)
            merged = term if i == 0 else merged + term
        mh[pl.ds(256 * p, 256)], ml[pl.ds(256 * p, 256)] = split(merged)
    send_h.wait_recv()
    gmat[pl.ds(0, 256), pl.ds(0, 256)] = hb[0]
    gmat[pl.ds(256, 256), pl.ds(256, 256)] = hb[1]
    _, alpha = weights(lambda n: None)
    ah, al = split(wf[...].T)
    bs[...] = alpha * dot3(ah, al, mh[...], ml[...])
    columns = pl.ds(pl.multiple_of(t * 256, 256), 256)
    final = [links.start(bs.at[rows(y_peer(d) * 64, 64)], out_ref.at[:, columns], at_y(d)) for d in range(1, N_TM)]
    out_ref[:, columns] = bs[rows(t * 64, 64)]
    wait(final)
    links.finish()


def share(links, spread, own, other, k, partner):
    for c in range(CHUNKS):
        for copy in spread[k, c]:
            copy.wait_recv()
    return links.start(own.at[k], other.at[k], partner)


def shards(terminal, goal_weight, conduct, active_count):
    n_space = lax.axis_size("space")
    n_z = n_space // (2 * NX_CHIPS)

    def f(*shape):
        return pltpu.VMEM(shape, F32)

    def h(*shape):
        return pltpu.VMEM(shape, BF16)

    scratch = [
        f(STEPS + 1, 8, GOALS, 128), f(8, GOALS, 128), f(STEPS, 8, GOALS, 128), f(STEPS, 8, GOALS, 128),
        f(STEPS, 2, 256, 128), f(STEPS, 2, 256, 128), h(4, 256, 512), h(4, 256, 512),
        f(1536, 128), f(1024, 128),
        f(3, 192, 128), f(3, 192, 128), f(192, 128), f(192, 128), f(3, 48, 128), f(3, 48, 128),
        f(128, 128), f(n_z - 1, 128 // n_z, 128), f(128, 128), f(192, 128), f(192, 128), f(1536, 128),
        f(3, 128, 128), f(3, 128, 128), f(128, 128), f(128, 128), f(3, 32, 128), f(3, 32, 128),
        f(64, 128), f(n_z - 1, 64 // n_z, 128), f(64, 128), f(128, 128), f(128, 128), f(2, 1024, 128),
        f(512, 512), f(512, 512), h(512, 512), h(512, 512), h(512, 512), h(512, 512), h(512, 512), h(512, 512),
        f(512, 256), h(512, 256), h(512, 256), h(512, 256), h(512, 256), f(512, 256), h(512, 256), h(512, 256),
        f(256, 512), f(2, 512, 256), f(2, 256, 256), h(512, 256), h(512, 256), f(8, 128), f(256, 256),
        pltpu.SemaphoreType.DMA((128,)), pltpu.SemaphoreType.DMA((128,)),
    ]
    vmem = pl.BlockSpec(memory_space=pltpu.VMEM)

    def body(*refs):
        kernel(n_space, *refs)

    return pl.pallas_call(
        body,
        out_shape=jax.ShapeDtypeStruct((256 // N_TM, 1024), F32),
        in_specs=[vmem, vmem, vmem, pl.BlockSpec(memory_space=pltpu.SMEM)],
        out_specs=vmem,
        scratch_shapes=scratch,
        compiler_params=pltpu.CompilerParams(
            collective_id=0, has_side_effects=True, vmem_limit_bytes=56 * 1024 * 1024),
        name="merge_tree",
    )(terminal.reshape(GOALS * 8, 128), goal_weight.reshape(GOALS * 8, 128), conduct.reshape(8, 128), active_count)


def solution(mesh):
    placed = (
        P("tm", None, "space", None, None),
        P(None, "space", None, None),
        P("space", None, None),
        P("tm"),
    )
    return jax.shard_map(
        shards, mesh=mesh, in_specs=placed, out_specs=P("tm", "space"), check_vma=False
    )
```

time: 589 us -> 103 us (0.17)
  waiting for transfers between devices: 488 us -> 0 us
  Pallas kernels: 0 us -> 100 us
  matrix products: 35.8 us -> 0 us
  starting transfers between devices: 29.1 us -> 0 us
  between operations: 18.4 us -> 0.66 us
  other arithmetic: 13.8 us -> 0 us
    psum x3 -> x0, waiting for transfers between devices: 430 us -> none  [the longest x2 381 us: merge_pair(): gram_matrix = lax.psum(outer_gram(stacked), 'space')]
    pallas_call x0 -> x1, Pallas kernels: none -> 100 us  [shards(): pl.pallas_call(body, out_shape=jax.ShapeDtypeStruct((256 // N_TM, 1024),...]
    ppermute x10 -> x0, waiting for transfers between devices: 58.9 us -> none  [the longest x2 45.9 us: from_behind(): lax.ppermute(value, axis, [(source, source + steps) for source in range(l...]
    dot_general x14 -> x0, matrix products: 35.8 us -> none  [the longest x10 21.9 us: product(): return jnp.dot(left, right, precision=lax.Precision.HIGHEST)]
    ppermute x10 -> x0, starting transfers between devices: 28.8 us -> none  [the longest x4 15.1 us: with_halo(): before = lax.ppermute(last, axis, up)]
    reduce_sum x4 -> x0, other arithmetic: 8.01 us -> none  [the longest x2 4.21 us: filter_weights(): sign_iter = shifted / jnp.sqrt(jnp.sum(shifted * shifted) + 1e-06)]
  transfers between devices with their start and end apart: 13 -> 0, of which waited for: 13 -> 0; matrix products, arithmetic and copies ran while one was open for 0% -> 0% of each run, Pallas kernels for 0% -> 0%
where the time goes in v1:
time: 103 us; the launch traced here: 102 us
  Pallas kernels  100 us (97%)
  local copies, waits for them, and re-layouts  1.67 us (2%)
    pallas_call x1, Pallas kernels, shards(): pl.pallas_call(body, out_shape=jax.ShapeDtypeStruct((256 // N_TM, 1024),...  100 us

profile of v1, /device:TPU:1, one launch (start us, length us, event | category | flops | bytes accessed | tf_op | source)
XLA Modules:
  0.0 102.5 jit_solution(5554505472466715349)
XLA Ops:
  0.7 100.1 %merge_tree.1 = f32[64,1024]{1,0:T(8,128)} custom-call(f32[512,128]{1,0:T(8,128)} %bitcast.3, f32[512,128]{1,0:T(8,128)} %bitcast.4, f32[8,128]{1,0:T(8,128)} %bitcast.5, s32[1]{0:T(128)S(6)} %copy.6.refs_3_), custom_call_target="tpu_custom_call" | custom-call | tf_op jit(solution)/shard_map/merge_tree/pallas_call | solution.py:409
  100.8 1.7 %copy.7 = f32[64,1024]{1,0:T(8,128)} copy(f32[64,1024]{1,0:T(8,128)} %merge_tree.1) | data formatting | bytes 524288

commit v2 on v1

--- a/solution.py
+++ b/solution.py
@@ -10,7 +10,7 @@
 LAYERS = 8
 NX_CHIPS = 4
 N_TM = 4
-CHUNKS = 2
+CHUNKS = 4
 F32 = jnp.float32
 BF16 = jnp.bfloat16
 
@@ -31,22 +31,45 @@
 NT = ((1,), (1,))
 
 
+class Arrival:
+    def __init__(self, sem, whole):
+        self.sem, self.whole, self.done = sem, whole, False
+
+    def wait(self):
+        self.done = True
+        pltpu.make_async_copy(self.whole, self.whole, self.sem).wait()
+
+
 class Links:
     def __init__(self, send_sems, recv_sems):
-        self.send_sems, self.recv_sems, self.copies = send_sems, recv_sems, []
-
-    def start(self, src, dst, device):
-        n = len(self.copies)
-        copy = pltpu.make_async_remote_copy(
-            src_ref=src, dst_ref=dst, send_sem=self.send_sems.at[n], recv_sem=self.recv_sems.at[n],
-            device_id=device, device_id_type=pl.DeviceIdType.MESH)
-        copy.start()
-        self.copies.append(copy)
-        return copy
+        self.send_sems, self.recv_sems, self.sent, self.arrivals = send_sems, recv_sems, [], []
+
+    def sending(self, whole):
+        sem = self.send_sems.at[len(self.sent)]
+        self.sent.append(Arrival(sem, whole))
+        return sem
+
+    def arrival(self, whole):
+        arrival = Arrival(self.recv_sems.at[len(self.arrivals)], whole)
+        self.arrivals.append(arrival)
+        return arrival
+
+    def group(self, copies, whole, send_sem=None):
+        if send_sem is None:
+            send_sem = self.sending(whole)
+        arrival = self.arrival(whole)
+        for src, dst, device in copies:
+            self.copy(src, dst, device, send_sem, arrival)
+        return arrival
+
+    def copy(self, src, dst, device, send_sem, arrival):
+        pltpu.make_async_remote_copy(
+            src_ref=src, dst_ref=dst, send_sem=send_sem, recv_sem=arrival.sem,
+            device_id=device, device_id_type=pl.DeviceIdType.MESH).start()
 
     def finish(self):
-        for copy in self.copies:
-            copy.wait_send()
+        for sent in self.sent:
+            sent.wait()
 
 
 def rows(start, size):
@@ -54,11 +77,11 @@
 
 
 def kernel(n_space, term_ref, goal_ref, cond_ref, count_ref, out_ref,
-           field, goal, halo_l, halo_r, own, other, sh, sl,
+           term_raw, goal_raw, in_sems, field, goal, halo, own, other, sh, sl,
            pg, pc, rx1, ry1, qx1, qy1, rx2, ry2, qz, rz, fz, q2x, q2y, gf,
            cx1, cy1, dx1, dy1, cx2, cy2, ez, crz, cfz, d2x, d2y, cb,
            gmat, s0f, s0h, s0l, zh, zl, s1h, s1l, ff, fh, fl, th, tl, wf, wh, wl, wt,
-           wb, hb, mh, ml, g2, bs, send_sems, recv_sems):
+           wb, hb, mh, ml, bs, send_sems, recv_sems):
     s = lax.axis_index("space")
     t = lax.axis_index("tm")
     core = s % 2
@@ -94,68 +117,82 @@
     for peer in peers:
         pl.semaphore_signal(barrier, inc=1, device_id=peer, device_id_type=pl.DeviceIdType.MESH)
 
+    size = GOALS // CHUNKS
+    loads = [pltpu.make_async_copy(term_ref, term_raw, in_sems.at[0]),
+             pltpu.make_async_copy(goal_ref, goal_raw, in_sems.at[1])]
+    for load in loads:
+        load.start()
     lane = lax.broadcasted_iota(jnp.int32, (1, 128), 1)
     mask = (lane // (128 // LAYERS) < count_ref[0]).astype(F32)
+    loads[0].wait()
     for y in range(8):
-        field[0, y] = term_ref[pl.ds(y, GOALS, stride=8), :] * mask
-        goal[y] = goal_ref[pl.ds(y, GOALS, stride=8), :] * mask
+        for c in range(CHUNKS):
+            field[0, c, y] = term_raw[pl.ds(c * size * 8 + y, size, stride=8), :] * mask
     pl.semaphore_wait(barrier, len(peers))
 
     links = Links(send_sems, recv_sems)
-    size = GOALS // CHUNKS
-
-    def part(c):
-        return pl.ds(c * size, size)
+
+    halo_sem = links.sending(halo)
+    spread_sem = links.sending(own.at[:, pl.ds(0, N_TM - 1)])
+    share_sem = links.sending(own)
 
     def send_halo(k, c):
-        to_right = links.start(field.at[k, :, part(c)], halo_l.at[k, :, part(c)], right)
-        to_left = links.start(field.at[k, :, part(c)], halo_r.at[k, :, part(c)], left)
-        return to_right, to_left
+        return links.group([(field.at[k, c], halo.at[k, c, 0], right), (field.at[k, c], halo.at[k, c, 1], left)],
+                           halo.at[k, c], halo_sem)
 
     has_left = jnp.where(s > 0, 1.0, 0.0).astype(F32)
     has_right = jnp.where(s < n_space - 1, 1.0, 0.0).astype(F32)
     inner_lo = (lane > 0).astype(F32)
     inner_hi = (lane < 127).astype(F32)
     halos = {(0, c): send_halo(0, c) for c in range(CHUNKS)}
-    spread = {}
-
-    def absorb(k):
-        for ref, base in ((own, 0), (other, 256)):
-            for yy in range(2):
-                for b in range(N_TM):
-                    high, low = split(ref[k, yy, pl.ds(b * GOALS, GOALS), :])
-                    sh[b, pl.ds(k * GOALS, GOALS), pl.ds(base + yy * 128, 128)] = high
-                    sl[b, pl.ds(k * GOALS, GOALS), pl.ds(base + yy * 128, 128)] = low
+    loads[1].wait()
+    for y in range(8):
+        for c in range(CHUNKS):
+            goal[c, y] = goal_raw[pl.ds(c * size * 8 + y, size, stride=8), :] * mask
+    spread = [links.arrival(own.at[k, pl.ds(0, N_TM - 1)]) for k in range(STEPS)]
+
+    def absorb(ref, base, k):
+        for yy in range(2):
+            for b in range(N_TM):
+                high, low = split(ref[k, b, :, yy].reshape(GOALS, 128))
+                sh[b, pl.ds(k * GOALS, GOALS), pl.ds(base + yy * 128, 128)] = high
+                sl[b, pl.ds(k * GOALS, GOALS), pl.ds(base + yy * 128, 128)] = low
+
+    def share(k):
+        spread[k].wait()
+        return links.group([(own.at[k], other.at[k], partner)], other.at[k], share_sem)
 
     shared = {}
     for k in range(STEPS):
         for c in range(CHUNKS):
-            for copy in halos[k, c]:
-                copy.wait_recv()
+            halos[k, c].wait()
             for y in range(8):
-                here = field[k, y, part(c)]
-                total = halo_l[k, y, part(c)] * has_left + halo_r[k, y, part(c)] * has_right
+                here = field[k, c, y]
+                total = halo[k, c, 0, y] * has_left + halo[k, c, 1, y] * has_right
                 if y > 0:
-                    total = total + field[k, y - 1, part(c)]
+                    total = total + field[k, c, y - 1]
                 if y < 7:
-                    total = total + field[k, y + 1, part(c)]
+                    total = total + field[k, c, y + 1]
                 total = total + pltpu.roll(here, 1, 1) * inner_lo + pltpu.roll(here, 127, 1) * inner_hi
                 kappa = cond_ref[pl.ds(y, 1), :]
-                field[k + 1, y, part(c)] = mask * (
-                    here + kappa * (total - 6.0 * here)) + goal[y, part(c)]
+                field[k + 1, c, y] = mask * (here + kappa * (total - 6.0 * here)) + goal[c, y]
             if k + 1 < STEPS:
                 halos[k + 1, c] = send_halo(k + 1, c)
-            spread[k, c] = [
-                links.start(field.at[k + 1, pl.ds(2 * y_peer(d), 2), part(c)],
-                            own.at[k, :, rows(t * GOALS + c * size, size)], at_y(d))
-                for d in range(1, N_TM)]
-            own[k, :, rows(t * GOALS + c * size, size)] = field[k + 1, pl.ds(2 * t, 2), part(c)]
+            for d in (2, 1, 3):
+                links.copy(field.at[k + 1, c, pl.ds(2 * y_peer(d), 2)], own.at[k, t, c], at_y(d), spread_sem, spread[k])
+            own[k, t, c] = field[k + 1, c, pl.ds(2 * t, 2)]
         if k > 0:
-            shared[k - 1] = share(links, spread, own, other, k - 1, partner)
-    shared[STEPS - 1] = share(links, spread, own, other, STEPS - 1, partner)
-    for k in range(STEPS):
-        shared[k].wait_recv()
-        absorb(k)
+            shared[k - 1] = share(k - 1)
+            absorb(own, 0, k - 1)
+        if k > 1:
+            shared[k - 2].wait()
+            absorb(other, 256, k - 2)
+    shared[STEPS - 1] = share(STEPS - 1)
+    shared[STEPS - 2].wait()
+    absorb(other, 256, STEPS - 2)
+    absorb(own, 0, STEPS - 1)
+    shared[STEPS - 1].wait()
+    absorb(other, 256, STEPS - 1)
 
     lower, upper = 2 * core, 2 * core + 1
 
@@ -171,23 +208,23 @@
         pc[pl.ds(n * 512, 256)] = g[:, :128]
         pc[pl.ds(n * 512 + 256, 256)] = g[:, 128:]
 
+    def offsets(count):
+        return sorted(range(1, count), key=lambda d: -min(d, count - d))
+
     def scatter(src, base, land, length, peer, at, count):
-        return [links.start(src.at[rows(base + peer(d) * length, length)], land.at[d - 1], at(d))
-                for d in range(1, count)]
-
-    def reduced(src, base, land, length, copies, place):
+        return links.group([(src.at[rows(base + peer(d) * length, length)], land.at[d - 1], at(d))
+                            for d in offsets(count)], land)
+
+    def reduced(src, base, land, length, arrival, place):
         total = src[rows(base + place * length, length)]
-        for d, copy in enumerate(copies):
-            copy.wait_recv()
+        arrival.wait()
+        for d in range(land.shape[0]):
             total = total + land[d]
         return total
 
     def gather(src, dst, base, length, place, at, count):
-        return [links.start(src, dst.at[rows(base + place * length, length)], at(d)) for d in range(1, count)]
-
-    def wait(copies):
-        for copy in copies:
-            copy.wait_recv()
+        return links.group([(src, dst.at[rows(base + place * length, length)], at(d)) for d in offsets(count)],
+                           dst.at[pl.ds(base, (count - 1) * length)])
 
     def stage1(src, landx, landy):
         half = src.shape[0] // 2
@@ -215,7 +252,7 @@
         return gather(full.at[rows(cz * length, length)], full, 0, length, cz, at_z, n_z)
 
     def back2(full, copies, qx, qy):
-        wait(copies)
+        copies.wait()
         length = qx.shape[0] // 4
         first = gather(full.at[pl.ds(0, length)], qx, 0, length, t, at_y, N_TM)
         second = gather(full.at[pl.ds(length, length)], qy, 0, length, cx, at_x, NX_CHIPS)
@@ -225,27 +262,29 @@
 
     def back3(qx, qy, copies, dst):
         length = qx.shape[0]
-        wait(copies[0])
+        copies[0].wait()
         first = gather(qx, dst, 0, length, cx, at_x, NX_CHIPS)
-        wait(copies[1])
+        copies[1].wait()
         second = gather(qy, dst, 4 * length, length, t, at_y, N_TM)
         dst[rows(cx * length, length)] = qx[...]
         dst[rows(4 * length + t * length, length)] = qy[...]
-        return first + second
-
+        return first, second
+
+    cmat = cb.at[core]
     g1 = stage1(pg, rx1, ry1)
+    c1 = stage1(pc, cx1, cy1)
     g2c = stage2(pg, rx1, ry1, g1, qx1, qy1, rx2, ry2)
-    c1 = stage1(pc, cx1, cy1)
+    c2 = stage2(pc, cx1, cy1, c1, dx1, dy1, cx2, cy2)
     g3 = stage3(qx1, qy1, rx2, ry2, g2c, qz, rz)
-    c2 = stage2(pc, cx1, cy1, c1, dx1, dy1, cx2, cy2)
+    c3 = stage3(dx1, dy1, cx2, cy2, c2, ez, crz)
     g4 = back1(qz, rz, g3, fz)
+    c4 = back1(ez, crz, c3, cfz)
     g5 = back2(fz, g4, q2x, q2y)
-    c3 = stage3(dx1, dy1, cx2, cy2, c2, ez, crz)
+    c5 = back2(cfz, c4, d2x, d2y)
     g6 = back3(q2x, q2y, g5, gf)
-    c4 = back1(ez, crz, c3, cfz)
-    wait(g6)
-
-    cmat = cb.at[core]
+    c6 = back3(d2x, d2y, c5, cmat)
+    for arrival in g6:
+        arrival.wait()
 
     def eye(size):
         return (lax.broadcasted_iota(jnp.int32, (size, size), 0)
@@ -310,34 +349,29 @@
             gw = wf[r] + norm * dot3(s0h[r], s0l[r], wh[...], wl[...])
             ff[r] = gw
             kept = kept + jnp.sum(wf[r] * gw)
-        ratio = 256.0 * energy / (energy * kept + 1e-6)
-        alpha = jnp.sqrt(energy * ratio / energy)
-        return energy, alpha
+        return energy, jnp.sqrt(256.0 * energy / (energy * kept + 1e-6))
 
     state = {}
 
     def between(n):
-        if n == 0:
-            state["c5"] = back2(cfz, c4, d2x, d2y)
         if n == 1:
-            state["c6"] = back3(d2x, d2y, state["c5"], cmat)
-        if n == 2:
-            wait(state["c6"])
-            state["c7"] = links.start(cmat, cmat, partner)
+            for arrival in c6:
+                arrival.wait()
+            state["c7"] = links.group([(cmat, cmat, partner)], cmat)
 
     energy, alpha = weights(between)
     for i in range(2):
         wf[pl.ds(256 * i, 256)] = wf[pl.ds(256 * i, 256)] * alpha
     wb[core] = wf[...]
-    send_w = links.start(wb.at[core], wb.at[core], partner)
+    send_w = links.group([(wb.at[core], wb.at[core], partner)], wb.at[core])
     for i in range(2):
         fh[pl.ds(256 * i, 256)], fl[pl.ds(256 * i, 256)] = split(ff[pl.ds(256 * i, 256)])
     wt[...] = wf[...].T
     ah, al = split(wt[...])
     hb[core] = (energy * alpha) * dot3(ah, al, fh[...], fl[...])
-    send_h = links.start(hb.at[core], hb.at[core], partner)
-    state["c7"].wait_recv()
-    send_w.wait_recv()
+    send_h = links.group([(hb.at[core], hb.at[core], partner)], hb.at[core])
+    state["c7"].wait()
+    send_w.wait()
 
     w1h, w1l = split(wb[1])
     th[...] = w1h
@@ -358,30 +392,26 @@
             term = dot3(ah[:, 256 * i:256 * i + 256], al[:, 256 * i:256 * i + 256], block_h, block_l)
             merged = term if i == 0 else merged + term
         mh[pl.ds(256 * p, 256)], ml[pl.ds(256 * p, 256)] = split(merged)
-    send_h.wait_recv()
+    send_h.wait()
     gmat[pl.ds(0, 256), pl.ds(0, 256)] = hb[0]
     gmat[pl.ds(256, 256), pl.ds(256, 256)] = hb[1]
     _, alpha = weights(lambda n: None)
     ah, al = split(wf[...].T)
     bs[...] = alpha * dot3(ah, al, mh[...], ml[...])
     columns = pl.ds(pl.multiple_of(t * 256, 256), 256)
-    final = [links.start(bs.at[rows(y_peer(d) * 64, 64)], out_ref.at[:, columns], at_y(d)) for d in range(1, N_TM)]
+    final = links.group([(bs.at[rows(y_peer(d) * 64, 64)], out_ref.at[:, columns], at_y(d)) for d in (2, 1, 3)],
+                        out_ref.at[:, pl.ds(0, 768)])
     out_ref[:, columns] = bs[rows(t * 64, 64)]
-    wait(final)
+    final.wait()
     links.finish()
-
-
-def share(links, spread, own, other, k, partner):
-    for c in range(CHUNKS):
-        for copy in spread[k, c]:
-            copy.wait_recv()
-    return links.start(own.at[k], other.at[k], partner)
 
 
 def shards(terminal, goal_weight, conduct, active_count):
     n_space = lax.axis_size("space")
     n_z = n_space // (2 * NX_CHIPS)
 
+    size = GOALS // CHUNKS
+
     def f(*shape):
         return pltpu.VMEM(shape, F32)
 
@@ -389,8 +419,10 @@
         return pltpu.VMEM(shape, BF16)
 
     scratch = [
-        f(STEPS + 1, 8, GOALS, 128), f(8, GOALS, 128), f(STEPS, 8, GOALS, 128), f(STEPS, 8, GOALS, 128),
-        f(STEPS, 2, 256, 128), f(STEPS, 2, 256, 128), h(4, 256, 512), h(4, 256, 512),
+        f(GOALS * 8, 128), f(GOALS * 8, 128), pltpu.SemaphoreType.DMA((2,)),
+        f(STEPS + 1, CHUNKS, 8, size, 128), f(CHUNKS, 8, size, 128),
+        f(STEPS, CHUNKS, 2, 8, size, 128),
+        f(STEPS, N_TM, CHUNKS, 2, size, 128), f(STEPS, N_TM, CHUNKS, 2, size, 128), h(4, 256, 512), h(4, 256, 512),
         f(1536, 128), f(1024, 128),
         f(3, 192, 128), f(3, 192, 128), f(192, 128), f(192, 128), f(3, 48, 128), f(3, 48, 128),
         f(128, 128), f(n_z - 1, 128 // n_z, 128), f(128, 128), f(192, 128), f(192, 128), f(1536, 128),
@@ -398,10 +430,11 @@
         f(64, 128), f(n_z - 1, 64 // n_z, 128), f(64, 128), f(128, 128), f(128, 128), f(2, 1024, 128),
         f(512, 512), f(512, 512), h(512, 512), h(512, 512), h(512, 512), h(512, 512), h(512, 512), h(512, 512),
         f(512, 256), h(512, 256), h(512, 256), h(512, 256), h(512, 256), f(512, 256), h(512, 256), h(512, 256),
-        f(256, 512), f(2, 512, 256), f(2, 256, 256), h(512, 256), h(512, 256), f(8, 128), f(256, 256),
-        pltpu.SemaphoreType.DMA((128,)), pltpu.SemaphoreType.DMA((128,)),
+        f(256, 512), f(2, 512, 256), f(2, 256, 256), h(512, 256), h(512, 256), f(256, 256),
+        pltpu.SemaphoreType.DMA((28,)), pltpu.SemaphoreType.DMA((50,)),
     ]
     vmem = pl.BlockSpec(memory_space=pltpu.VMEM)
+    place = pl.BlockSpec(memory_space=pl.ANY)
 
     def body(*refs):
         kernel(n_space, *refs)
@@ -409,7 +442,7 @@
     return pl.pallas_call(
         body,
         out_shape=jax.ShapeDtypeStruct((256 // N_TM, 1024), F32),
-        in_specs=[vmem, vmem, vmem, pl.BlockSpec(memory_space=pltpu.SMEM)],
+        in_specs=[place, place, vmem, pl.BlockSpec(memory_space=pltpu.SMEM)],
         out_specs=vmem,
         scratch_shapes=scratch,
         compiler_params=pltpu.CompilerParams(

time: 103 us -> 87.4 us (0.85)
  Pallas kernels: 100 us -> 84.9 us
    pallas_call x1, Pallas kernels: 100 us -> 84.9 us  [shards(): pl.pallas_call(body, out_shape=jax.ShapeDtypeStruct((256 // N_TM, 1024),...]
where the time goes in v2:
time: 87.4 us; the launch traced here: 87.3 us
  Pallas kernels  84.9 us (97%)
  local copies, waits for them, and re-layouts  1.67 us (2%)
    pallas_call x1, Pallas kernels, shards(): pl.pallas_call(body, out_shape=jax.ShapeDtypeStruct((256 // N_TM, 1024),...  84.9 us

profile of v2, /device:TPU:1, one launch (start us, length us, event | category | flops | bytes accessed | tf_op | source)
XLA Modules:
  0.0 87.3 jit_solution(9801139146698657615)
XLA Ops:
  0.7 84.9 %merge_tree.1 = f32[64,1024]{1,0:T(8,128)} custom-call(f32[512,128]{1,0:T(8,128)} %bitcast.3, f32[512,128]{1,0:T(8,128)} %bitcast.4, f32[8,128]{1,0:T(8,128)} %bitcast.5, s32[1]{0:T(128)S(6)} %copy.6.refs_3_), custom_call_target="tpu_custom_call" | custom-call | tf_op jit(solution)/shard_map/merge_tree/pallas_call | solution.py:442
  85.6 1.7 %copy.7 = f32[64,1024]{1,0:T(8,128)} copy(f32[64,1024]{1,0:T(8,128)} %merge_tree.1) | data formatting | bytes 524288

commit v3 on v2

v3 whole, which is shorter than its diff:
```python
import jax
import jax.numpy as jnp
from jax import lax
from jax.experimental import pallas as pl
from jax.experimental.pallas import tpu as pltpu
from jax.sharding import PartitionSpec as P

STEPS = 4
GOALS = 64
LAYERS = 8
NX_CHIPS = 4
N_TM = 4
CHUNKS = 8
GROUPS = 4
F32 = jnp.float32
BF16 = jnp.bfloat16


def split(x):
    high = x.astype(BF16)
    return high, (x - high.astype(F32)).astype(BF16)


def dot(a, b, dims):
    return lax.dot_general(a, b, (dims, ((), ())), preferred_element_type=F32)


def dot3(ah, al, bh, bl, dims=((1,), (0,))):
    return dot(ah, bh, dims) + (dot(ah, bl, dims) + dot(al, bh, dims))


NT = ((1,), (1,))


class Arrival:
    def __init__(self, sem, whole):
        self.sem, self.whole, self.done = sem, whole, False

    def wait(self):
        self.done = True
        pltpu.make_async_copy(self.whole, self.whole, self.sem).wait()


class Links:
    def __init__(self, send_sems, recv_sems):
        self.send_sems, self.recv_sems, self.sent, self.arrivals = send_sems, recv_sems, [], []

    def sending(self, whole):
        sem = self.send_sems.at[len(self.sent)]
        self.sent.append(Arrival(sem, whole))
        return sem

    def arrival(self, whole):
        arrival = Arrival(self.recv_sems.at[len(self.arrivals)], whole)
        self.arrivals.append(arrival)
        return arrival

    def group(self, copies, whole, send_sem=None):
        if send_sem is None:
            send_sem = self.sending(whole)
        arrival = self.arrival(whole)
        for src, dst, device in copies:
            self.copy(src, dst, device, send_sem, arrival)
        return arrival

    def copy(self, src, dst, device, send_sem, arrival):
        pltpu.make_async_remote_copy(
            src_ref=src, dst_ref=dst, send_sem=send_sem, recv_sem=arrival.sem,
            device_id=device, device_id_type=pl.DeviceIdType.MESH).start()

    def finish(self):
        for sent in self.sent:
            sent.wait()


def rows(start, size):
    return pl.ds(pl.multiple_of(start, 8), size)


def kernel(n_space, term_ref, goal_ref, cond_ref, count_ref, out_ref,
           term_raw, goal_raw, in_sems, field, goal, halo, own, other, sh, sl,
           pe, pg, pc, ee, ge, cb, *rest):
    early_bufs, pair_bufs, cross_bufs = rest[:10], rest[10:20], rest[20:30]
    (s0f, s0h, s0l, zh, zl, s1h, s1l, ff, fh, fl, th, tl, wf, wh, wl,
           wb, hb, mh, ml, ph, pw, bs, land, send_sems, recv_sems) = rest[30:]
    s = lax.axis_index("space")
    t = lax.axis_index("tm")
    core = s % 2
    chip = s // 2
    cx = chip % NX_CHIPS
    cz = chip // NX_CHIPS
    n_z = n_space // (2 * NX_CHIPS)
    left = (lax.rem(s + n_space - 1, n_space), t)
    right = (lax.rem(s + 1, n_space), t)
    partner = (s + 1 - 2 * core, t)

    def y_peer(d):
        return lax.rem(t + d, N_TM)

    def x_peer(d):
        return lax.rem(cx + d, NX_CHIPS)

    def z_peer(d):
        return lax.rem(cz + d, n_z)

    def at_y(d):
        return (s, y_peer(d))

    def at_x(d):
        return ((cz * NX_CHIPS + x_peer(d)) * 2 + core, t)

    def at_z(d):
        return ((z_peer(d) * NX_CHIPS + cx) * 2 + core, t)

    peers = [left, right] + [at_y(d) for d in range(1, N_TM)] + [at_x(d) for d in range(1, NX_CHIPS)]
    peers += [at_z(d) for d in range(1, n_z)]
    barrier = pltpu.get_barrier_semaphore()
    for peer in peers:
        pl.semaphore_signal(barrier, inc=1, device_id=peer, device_id_type=pl.DeviceIdType.MESH)

    size = GOALS // CHUNKS
    loads = [pltpu.make_async_copy(term_ref, term_raw, in_sems.at[0]),
             pltpu.make_async_copy(goal_ref, goal_raw, in_sems.at[1])]
    for load in loads:
        load.start()
    lane = lax.broadcasted_iota(jnp.int32, (1, 128), 1)
    mask = (lane // (128 // LAYERS) < count_ref[0]).astype(F32)
    loads[0].wait()
    for y in range(8):
        for c in range(CHUNKS):
            field[0, c, y] = term_raw[pl.ds(c * size * 8 + y, size, stride=8), :] * mask
    pl.semaphore_wait(barrier, len(peers))

    links = Links(send_sems, recv_sems)

    halo_sem = links.sending(halo)
    spread_sem = links.sending(own.at[:, pl.ds(0, N_TM - 1)])
    share_sem = links.sending(own)

    def send_halo(k, c):
        return links.group([(field.at[k, c], halo.at[k, c, 0], right), (field.at[k, c], halo.at[k, c, 1], left)],
                           halo.at[k, c], halo_sem)

    def offsets(count):
        return sorted(range(1, count), key=lambda d: -min(d, count - d))

    def scatter(src, base, land, length, peer, at, count):
        return links.group([(src.at[rows(base + peer(d) * length, length)], land.at[d - 1], at(d))
                            for d in offsets(count)], land)

    def reduced(src, base, land, length, arrival, place):
        total = src[rows(base + place * length, length)]
        arrival.wait()
        for d in range(land.shape[0]):
            total = total + land[d]
        return total

    def gather(src, dst, base, length, place, at, count):
        return links.group([(src, dst.at[rows(base + place * length, length)], at(d)) for d in offsets(count)],
                           dst.at[pl.ds(base, (count - 1) * length)])

    def stage1(src, bufs):
        landx, landy = bufs[:2]
        half = src.shape[0] // 2
        return (scatter(src, 0, landx, half // 4, x_peer, at_x, NX_CHIPS),
                scatter(src, half, landy, half // 4, y_peer, at_y, N_TM))

    def stage2(src, bufs, copies):
        landx, landy, qx, qy, landx2, landy2 = bufs[:6]
        half = src.shape[0] // 2
        qx[...] = reduced(src, 0, landx, half // 4, copies[0], cx)
        first = scatter(qx, 0, landx2, half // 16, y_peer, at_y, N_TM)
        qy[...] = reduced(src, half, landy, half // 4, copies[1], t)
        return first, scatter(qy, 0, landy2, half // 16, x_peer, at_x, NX_CHIPS)

    def stage3(bufs, copies):
        qx, qy, landx2, landy2, q, land = bufs[2:8]
        length = qx.shape[0] // 4
        q[pl.ds(0, length)] = reduced(qx, 0, landx2, length, copies[0], t)
        q[pl.ds(length, length)] = reduced(qy, 0, landy2, length, copies[1], cx)
        if q.shape[0] > 2 * length:
            q[pl.ds(2 * length, q.shape[0] - 2 * length)] = jnp.zeros((q.shape[0] - 2 * length, 128), F32)
        return scatter(q, 0, land, q.shape[0] // n_z, z_peer, at_z, n_z)

    def back1(bufs, copies):
        q, land, full = bufs[6:9]
        length = q.shape[0] // n_z
        full[rows(cz * length, length)] = reduced(q, 0, land, length, copies, cz)
        return gather(full.at[rows(cz * length, length)], full, 0, length, cz, at_z, n_z)

    def back2(bufs, copies):
        full = bufs[8]
        qx, qy = bufs[9].at[0], bufs[9].at[1]
        copies.wait()
        length = qx.shape[0] // 4
        first = gather(full.at[pl.ds(0, length)], qx, 0, length, t, at_y, N_TM)
        second = gather(full.at[pl.ds(length, length)], qy, 0, length, cx, at_x, NX_CHIPS)
        qx[rows(t * length, length)] = full[pl.ds(0, length)]
        qy[rows(cx * length, length)] = full[pl.ds(length, length)]
        return first, second

    def back3(bufs, copies, dst):
        qx, qy = bufs[9].at[0], bufs[9].at[1]
        length = qx.shape[0]
        copies[0].wait()
        first = gather(qx, dst, 0, length, cx, at_x, NX_CHIPS)
        copies[1].wait()
        second = gather(qy, dst, 4 * length, length, t, at_y, N_TM)
        dst[rows(cx * length, length)] = qx[...]
        dst[rows(4 * length + t * length, length)] = qy[...]
        return first, second

    has_left = jnp.where(s > 0, 1.0, 0.0).astype(F32)
    has_right = jnp.where(s < n_space - 1, 1.0, 0.0).astype(F32)
    inner_lo = (lane > 0).astype(F32)
    inner_hi = (lane < 127).astype(F32)
    halos = {(0, c): send_halo(0, c) for c in range(CHUNKS)}
    loads[1].wait()
    for y in range(8):
        for c in range(CHUNKS):
            goal[c, y] = goal_raw[pl.ds(c * size * 8 + y, size, stride=8), :] * mask
    final_step, each = STEPS - 1, CHUNKS // GROUPS
    spread = [links.arrival(own.at[k, pl.ds(0, N_TM - 1)]) for k in range(final_step)]
    last_spread = [links.arrival(own.at[final_step, pl.ds(0, N_TM - 1), pl.ds(g * each, each)])
                   for g in range(GROUPS)]

    def absorb(ref, base, k, c, count):
        for yy in range(2):
            for b in range(N_TM):
                high, low = split(ref[k, b, pl.ds(c, count), yy].reshape(count * size, 128))
                place = pl.ds(k * GOALS + c * size, count * size)
                sh[b, place, pl.ds(base + yy * 128, 128)] = high
                sl[b, place, pl.ds(base + yy * 128, 128)] = low

    def share(arrival, k, c, count):
        arrival.wait()
        some = (k, slice(None), pl.ds(c, count))
        return links.group([(own.at[some], other.at[some], partner)], other.at[some], share_sem)

    shared = {}
    for k in range(STEPS):
        for c in range(CHUNKS):
            halos[k, c].wait()
            for y in range(8):
                here = field[k, c, y]
                total = halo[k, c, 0, y] * has_left + halo[k, c, 1, y] * has_right
                if y > 0:
                    total = total + field[k, c, y - 1]
                if y < 7:
                    total = total + field[k, c, y + 1]
                total = total + pltpu.roll(here, 1, 1) * inner_lo + pltpu.roll(here, 127, 1) * inner_hi
                kappa = cond_ref[pl.ds(y, 1), :]
                field[k + 1, c, y] = mask * (here + kappa * (total - 6.0 * here)) + goal[c, y]
            if k + 1 < STEPS:
                halos[k + 1, c] = send_halo(k + 1, c)
            for d in (2, 1, 3):
                links.copy(field.at[k + 1, c, pl.ds(2 * y_peer(d), 2)], own.at[k, t, c], at_y(d), spread_sem,
                           spread[k] if k < final_step else last_spread[c // each])
            own[k, t, c] = field[k + 1, c, pl.ds(2 * t, 2)]
        if k > 0:
            shared[k - 1] = share(spread[k - 1], k - 1, 0, CHUNKS)
            absorb(own, 0, k - 1, 0, CHUNKS)
        if k > 1:
            shared[k - 2].wait()
            absorb(other, 256, k - 2, 0, CHUNKS)
    shared[final_step - 1].wait()
    absorb(other, 256, final_step - 1, 0, CHUNKS)

    lower, upper = 2 * core, 2 * core + 1
    first, second = pl.ds(0, 128), pl.ds(128, 128)

    def both(ref, i, j):
        return jnp.concatenate([ref[i, first], ref[j, first]], 0)

    def early(i, j, k):
        return dot3(sh[i, first], sl[i, first], both(sh, j, k), both(sl, j, k), NT)

    g = early(lower, lower, upper)
    pe[pl.ds(0, 128)] = g[:, :128]
    pe[pl.ds(128, 128)] = g[:, 128:]
    g = dot3(sh[upper, first], sl[upper, first], sh[upper, first], sl[upper, first], NT)
    pe[pl.ds(256, 128)] = g
    g = early(core, 2, 3)
    pe[pl.ds(384, 128)] = g[:, :128]
    pg[pl.ds(896, 128)] = g[:, 128:]
    e1 = stage1(pe, early_bufs)
    last_shared = []
    for g in range(GROUPS):
        last_shared.append(share(last_spread[g], final_step, g * each, each))
        absorb(own, 0, final_step, g * each, each)
    for g in range(GROUPS):
        last_shared[g].wait()
        absorb(other, 256, final_step, g * each, each)

    e2 = stage2(pe, early_bufs, e1)

    def put(ref, n, value):
        ref[pl.ds(128 * n, 128)] = value

    def late(n, i):
        g = dot3(sh[i, second], sl[i, second], sh[i], sl[i], NT)
        put(pg, n, g[:, :128])
        put(pg, n + 1, g[:, 128:])

    def mixed(ref, n, i, j):
        g = dot3(sh[i], sl[i], sh[j], sl[j], NT)
        put(ref, n, g[:128, 128:])
        put(ref, n + 1, g[128:, :128])
        put(ref, n + 2, g[128:, 128:])

    late(0, lower)
    mixed(pg, 2, lower, upper)
    late(5, upper)
    g1 = stage1(pg, pair_bufs)
    mixed(pc, 0, core, 2)
    mixed(pc, 3, core, 3)

    cmat = cb.at[core, pl.ds(0, 768)]
    c1 = stage1(pc, cross_bufs)
    e3 = stage3(early_bufs, e2)
    g2 = stage2(pg, pair_bufs, g1)
    c2 = stage2(pc, cross_bufs, c1)
    e4 = back1(early_bufs, e3)
    g3 = stage3(pair_bufs, g2)
    c3 = stage3(cross_bufs, c2)
    e5 = back2(early_bufs, e4)
    g4 = back1(pair_bufs, g3)
    c4 = back1(cross_bufs, c3)
    e6 = back3(early_bufs, e5, ee)
    g5 = back2(pair_bufs, g4)
    c5 = back2(cross_bufs, c4)
    g6 = back3(pair_bufs, g5, ge)
    c6 = back3(cross_bufs, c5, cmat)
    for arrival in e6:
        arrival.wait()
    for arrival in g6:
        arrival.wait()

    identity = (lax.broadcasted_iota(jnp.int32, (256, 256), 0)
                == lax.broadcasted_iota(jnp.int32, (256, 256), 1)).astype(F32)
    halves = (pl.ds(0, 256), pl.ds(256, 256))

    def square(upper_left, lower_left, lower_right):
        top = jnp.concatenate([upper_left, lower_left.T], 1)
        return jnp.concatenate([top, jnp.concatenate([lower_left, lower_right], 1)], 0)

    def tile(ref, n):
        return ref[pl.ds(128 * n, 128)]

    def put_s0(i, j, value):
        s0f[halves[i], halves[j]] = value
        s0h[halves[i], halves[j]], s0l[halves[i], halves[j]] = split(value)

    def weights(g00, g01, g11):
        energy = jnp.sum((g00 + g11) * identity) / 512.0 + 1e-6
        inverse = 1.0 / energy
        upper, lower_, across = g00 * inverse - identity, g11 * inverse - identity, g01 * inverse
        put_s0(0, 0, upper)
        put_s0(1, 1, lower_)
        put_s0(0, 1, across)
        put_s0(1, 0, across.T)
        norm2 = jnp.sum(upper * upper + lower_ * lower_ + 2.0 * (across * across)) + 1e-6
        scale = 1.0 / jnp.sqrt(norm2)
        for r in halves:
            zh[r], zl[r] = split(dot3(s0h[r], s0l[r], s0h[...], s0l[...]))
        folded = None
        for r in halves:
            s1 = (1.5 * scale) * s0f[r] - (0.5 * scale / norm2) * dot3(s0h[r], s0l[r], zh[...], zl[...])
            s1h[r], s1l[r] = split(s1)
            folded = s1 if folded is None else folded + s1
        ff[...] = folded
        fh[...], fl[...] = split(folded)
        th[...], tl[...] = split(dot3(fh[...], fl[...], s1h[...], s1l[...]))
        u = dot3(th[...], tl[...], s1h[...], s1l[...])
        w = (jnp.concatenate([identity, identity], 1) + 1.5 * ff[...] - 0.5 * u) * (0.5 / 2.0 ** 0.5)
        wf[...] = w
        wh[...], wl[...] = split(w)
        return energy

    def kept_part(energy):
        gw = wf[...] + dot3(wh[...], wl[...], s0h[...], s0l[...])
        ff[...] = gw
        kept = energy * jnp.sum(wf[...] * gw)
        return jnp.sqrt(energy * 256.0 / (kept + 1e-6))

    energy = weights(
        square(tile(ee, 0), tile(ge, 0), tile(ge, 1)),
        jnp.concatenate([jnp.concatenate([tile(ee, 1), tile(ge, 2)], 1),
                         jnp.concatenate([tile(ge, 3), tile(ge, 4)], 1)], 0),
        square(tile(ee, 2), tile(ge, 5), tile(ge, 6)))
    wb[core] = wf[...]
    send_w = links.group([(wb.at[core], wb.at[core], partner)], wb.at[core])
    for arrival in c6:
        arrival.wait()
    cb[core, pl.ds(768, 128)] = tile(ee, 3)
    cb[core, pl.ds(896, 128)] = tile(ge, 7)
    send_c = links.group([(cb.at[core], cb.at[core], partner)], cb.at[core])
    alpha = kept_part(energy)
    fh[...], fl[...] = split(ff[...])
    hb[core, pl.ds(0, 256)] = (energy * alpha * alpha) * dot3(fh[...], fl[...], wh[...], wl[...], NT)
    hb[core, pl.ds(256, 8)] = jnp.full((8, 256), alpha, F32)
    send_h = links.group([(hb.at[core], hb.at[core], partner)], hb.at[core])
    send_w.wait()

    merged = []
    for p in range(2):
        wh[...], wl[...] = split(wb[p])
        terms = [dot3(wh[:, 256 * i:256 * i + 256], wl[:, 256 * i:256 * i + 256],
                      sh[2 * p + i, :, pl.ds(0, 256)], sl[2 * p + i, :, pl.ds(0, 256)]) for i in range(2)]
        merged.append(terms[0] + terms[1])
    send_c.wait()
    for i in range(2):
        c_rows = jnp.concatenate([jnp.concatenate([cb[i, pl.ds(128 * n, 128)] for n in order], 1)
                                  for order in ((6, 0, 7, 3), (1, 2, 4, 5))], 0)
        ch, cl = split(c_rows)
        ph[halves[i]], pw[halves[i]] = split(dot3(ch, cl, wh[...], wl[...], NT))
    wh[...], wl[...] = split(wb[0])
    cross = dot3(wh[...], wl[...], ph[...], pw[...])
    send_h.wait()
    alphas = [hb[p, pl.ds(256, 1)] for p in range(2)]
    for p in range(2):
        mh[halves[p]], ml[halves[p]] = split(merged[p] * alphas[p])
    energy = weights(hb[0, pl.ds(0, 256)], cross * (alphas[0] * alphas[1]), hb[1, pl.ds(0, 256)])
    bs[...] = dot3(wh[...], wl[...], mh[...], ml[...])
    columns = pl.ds(pl.multiple_of(t * 256, 256), 256)
    final = links.group([(bs.at[rows(y_peer(d) * 64, 64)], land.at[:, columns], at_y(d)) for d in (2, 1, 3)],
                        land.at[:, pl.ds(0, 768)])
    land[:, columns] = bs[rows(t * 64, 64)]
    alpha = kept_part(energy)
    final.wait()
    out_ref[...] = alpha * land[...]
    links.finish()


def shards(terminal, goal_weight, conduct, active_count):
    n_space = lax.axis_size("space")
    n_z = n_space // (2 * NX_CHIPS)

    size = GOALS // CHUNKS

    def f(*shape):
        return pltpu.VMEM(shape, F32)

    def h(*shape):
        return pltpu.VMEM(shape, BF16)

    def stages(length):
        one, two = length // 8, length // 32
        pad = -(-2 * two // (8 * n_z)) * 8 * n_z
        return [f(3, one, 128), f(3, one, 128), f(one, 128), f(one, 128), f(3, two, 128), f(3, two, 128),
                f(pad, 128), f(n_z - 1, pad // n_z, 128), f(pad, 128), f(2, one, 128)]

    scratch = [
        f(GOALS * 8, 128), f(GOALS * 8, 128), pltpu.SemaphoreType.DMA((2,)),
        f(STEPS + 1, CHUNKS, 8, size, 128), f(CHUNKS, 8, size, 128),
        f(STEPS, CHUNKS, 2, 8, size, 128),
        f(STEPS, N_TM, CHUNKS, 2, size, 128), f(STEPS, N_TM, CHUNKS, 2, size, 128), h(4, 256, 512), h(4, 256, 512),
        f(512, 128), f(1024, 128), f(768, 128), f(512, 128), f(1024, 128), f(2, 1024, 128),
        *stages(512), *stages(1024), *stages(768),
        f(512, 512), h(512, 512), h(512, 512), h(512, 512), h(512, 512), h(512, 512), h(512, 512),
        f(256, 512), h(256, 512), h(256, 512), h(256, 512), h(256, 512), f(256, 512), h(256, 512), h(256, 512),
        f(2, 256, 512), f(2, 264, 256), h(512, 256), h(512, 256), h(512, 256), h(512, 256), f(256, 256), f(64, 1024),
        pltpu.SemaphoreType.DMA((37,)), pltpu.SemaphoreType.DMA((80,)),
    ]
    vmem = pl.BlockSpec(memory_space=pltpu.VMEM)
    place = pl.BlockSpec(memory_space=pl.ANY)

    def body(*refs):
        kernel(n_space, *refs)

    return pl.pallas_call(
        body,
        out_shape=jax.ShapeDtypeStruct((256 // N_TM, 1024), F32),
        in_specs=[place, place, vmem, pl.BlockSpec(memory_space=pltpu.SMEM)],
        out_specs=vmem,
        scratch_shapes=scratch,
        compiler_params=pltpu.CompilerParams(
            collective_id=0, has_side_effects=True, vmem_limit_bytes=32 * 1024 * 1024),
        name="merge_tree",
    )(terminal.reshape(GOALS * 8, 128), goal_weight.reshape(GOALS * 8, 128), conduct.reshape(8, 128), active_count)


def solution(mesh):
    placed = (
        P("tm", None, "space", None, None),
        P(None, "space", None, None),
        P("space", None, None),
        P("tm"),
    )
    return jax.shard_map(
        shards, mesh=mesh, in_specs=placed, out_specs=P("tm", "space"), check_vma=False
    )
```

time: 87.4 us -> 84.2 us (0.963)
  Pallas kernels: 84.9 us -> 80.8 us
  local copies, waits for them, and re-layouts: 1.67 us -> 2.63 us
    pallas_call x1, Pallas kernels: 84.9 us -> 80.8 us  [shards(): pl.pallas_call(body, out_shape=jax.ShapeDtypeStruct((256 // N_TM, 1024),...]
    unnamed x1 -> x7, local copies, waits for them, and re-layouts: 1.67 us -> 2.63 us
where the time goes in v3:
time: 84.2 us; the launch traced here: 84.1 us
  Pallas kernels  80.8 us (96%)
  local copies, waits for them, and re-layouts  2.63 us (3%)
    pallas_call x1, Pallas kernels, shards(): pl.pallas_call(body, out_shape=jax.ShapeDtypeStruct((256 // N_TM, 1024),...  80.8 us
    unnamed x7, local copies, waits for them, and re-layouts  2.63 us

profile of v3, /device:TPU:1, one launch (start us, length us, event | category | flops | bytes accessed | tf_op | source)
XLA Modules:
  0.0 84.1 jit_solution(12207536407952455336)
XLA Ops:
  0.0 0.0 copy-start.2
  0.7 0.0 copy-done.2
  0.7 0.0 copy-start
  0.7 0.9 %copy-done = f32[1,64,1,8,128]{4,3,2,1,0:T(8,128)S(1)} copy-done((f32[1,64,1,8,128]{4,3,2,1,0:T(8,128)S(1)}, f32[1,64,1,8,128]{4,3,2,1,0:T(8,128)}, u32[]{:S(2)}) %copy-start) | copy-done | bytes 262168
  1.6 0.0 copy-start.1
  1.6 0.9 %copy-done.1 = f32[64,1,8,128]{3,2,1,0:T(8,128)S(1)} copy-done((f32[64,1,8,128]{3,2,1,0:T(8,128)S(1)}, f32[64,1,8,128]{3,2,1,0:T(8,128)}, u32[]{:S(2)}) %copy-start.1) | copy-done | bytes 262168
  2.6 80.8 %merge_tree.1 = f32[64,1024]{1,0:T(8,128)S(1)} custom-call(f32[512,128]{1,0:T(8,128)S(1)} %bitcast.3, f32[512,128]{1,0:T(8,128)S(1)} %bitcast.4, f32[8,128]{1,0:T(8,128)S(1)} %bitcast.5, s32[1]{0:T(128)S(6)} %copy.6.refs_3_), custom_call_target="tpu_custom_call" | custom-call | tf_op jit(solution)/shard_map/merge_tree/pallas_call | solution.py:471
  83.4 0.7 copy.7
Async XLA Ops:
  0.0 0.7 copy-start.2
  0.7 0.9 %copy-start = (f32[1,64,1,8,128]{4,3,2,1,0:T(8,128)S(1)}, f32[1,64,1,8,128]{4,3,2,1,0:T(8,128)}, u32[]{:S(2)}) copy-start(f32[1,64,1,8,128]{4,3,2,1,0:T(8,128)} %param.4) | copy-start | bytes 786436
  1.6 0.9 %copy-start.1 = (f32[64,1,8,128]{3,2,1,0:T(8,128)S(1)}, f32[64,1,8,128]{3,2,1,0:T(8,128)}, u32[]{:S(2)}) copy-start(f32[64,1,8,128]{3,2,1,0:T(8,128)} %param.5) | copy-start | bytes 786436

commit v4 on v3

--- a/solution.py
+++ b/solution.py
@@ -70,7 +70,8 @@
 
     def finish(self):
         for sent in self.sent:
-            sent.wait()
+            if not sent.done:
+                sent.wait()
 
 
 def rows(start, size):
@@ -351,8 +352,8 @@
         s0f[halves[i], halves[j]] = value
         s0h[halves[i], halves[j]], s0l[halves[i], halves[j]] = split(value)
 
-    def weights(g00, g01, g11):
-        energy = jnp.sum((g00 + g11) * identity) / 512.0 + 1e-6
+    def weights(g00, g01, g11, trace):
+        energy = trace / 512.0 + 1e-6
         inverse = 1.0 / energy
         upper, lower_, across = g00 * inverse - identity, g11 * inverse - identity, g01 * inverse
         put_s0(0, 0, upper)
@@ -381,13 +382,15 @@
         gw = wf[...] + dot3(wh[...], wl[...], s0h[...], s0l[...])
         ff[...] = gw
         kept = energy * jnp.sum(wf[...] * gw)
-        return jnp.sqrt(energy * 256.0 / (kept + 1e-6))
-
+        alpha = jnp.sqrt(energy * 256.0 / (kept + 1e-6))
+        return alpha, alpha * alpha * kept
+
+    trace = jnp.sum((tile(ee, 0) + tile(ge, 1) + tile(ee, 2) + tile(ge, 6)) * identity[:128, :128])
     energy = weights(
         square(tile(ee, 0), tile(ge, 0), tile(ge, 1)),
         jnp.concatenate([jnp.concatenate([tile(ee, 1), tile(ge, 2)], 1),
                          jnp.concatenate([tile(ge, 3), tile(ge, 4)], 1)], 0),
-        square(tile(ee, 2), tile(ge, 5), tile(ge, 6)))
+        square(tile(ee, 2), tile(ge, 5), tile(ge, 6)), trace)
     wb[core] = wf[...]
     send_w = links.group([(wb.at[core], wb.at[core], partner)], wb.at[core])
     for arrival in c6:
@@ -395,10 +398,11 @@
     cb[core, pl.ds(768, 128)] = tile(ee, 3)
     cb[core, pl.ds(896, 128)] = tile(ge, 7)
     send_c = links.group([(cb.at[core], cb.at[core], partner)], cb.at[core])
-    alpha = kept_part(energy)
+    alpha, trace = kept_part(energy)
     fh[...], fl[...] = split(ff[...])
     hb[core, pl.ds(0, 256)] = (energy * alpha * alpha) * dot3(fh[...], fl[...], wh[...], wl[...], NT)
     hb[core, pl.ds(256, 8)] = jnp.full((8, 256), alpha, F32)
+    hb[core, pl.ds(264, 8)] = jnp.full((8, 256), trace, F32)
     send_h = links.group([(hb.at[core], hb.at[core], partner)], hb.at[core])
     send_w.wait()
 
@@ -420,13 +424,16 @@
     alphas = [hb[p, pl.ds(256, 1)] for p in range(2)]
     for p in range(2):
         mh[halves[p]], ml[halves[p]] = split(merged[p] * alphas[p])
-    energy = weights(hb[0, pl.ds(0, 256)], cross * (alphas[0] * alphas[1]), hb[1, pl.ds(0, 256)])
+    energy = weights(hb[0, pl.ds(0, 256)], cross * (alphas[0] * alphas[1]), hb[1, pl.ds(0, 256)],
+                     jnp.sum(hb[0, pl.ds(264, 1), pl.ds(0, 1)] + hb[1, pl.ds(264, 1), pl.ds(0, 1)]))
     bs[...] = dot3(wh[...], wl[...], mh[...], ml[...])
     columns = pl.ds(pl.multiple_of(t * 256, 256), 256)
     final = links.group([(bs.at[rows(y_peer(d) * 64, 64)], land.at[:, columns], at_y(d)) for d in (2, 1, 3)],
                         land.at[:, pl.ds(0, 768)])
     land[:, columns] = bs[rows(t * 64, 64)]
-    alpha = kept_part(energy)
+    alpha = kept_part(energy)[0]
+    for sent in links.sent[:-1]:
+        sent.wait()
     final.wait()
     out_ref[...] = alpha * land[...]
     links.finish()
@@ -459,7 +466,7 @@
         *stages(512), *stages(1024), *stages(768),
         f(512, 512), h(512, 512), h(512, 512), h(512, 512), h(512, 512), h(512, 512), h(512, 512),
         f(256, 512), h(256, 512), h(256, 512), h(256, 512), h(256, 512), f(256, 512), h(256, 512), h(256, 512),
-        f(2, 256, 512), f(2, 264, 256), h(512, 256), h(512, 256), h(512, 256), h(512, 256), f(256, 256), f(64, 1024),
+        f(2, 256, 512), f(2, 272, 256), h(512, 256), h(512, 256), h(512, 256), h(512, 256), f(256, 256), f(64, 1024),
         pltpu.SemaphoreType.DMA((37,)), pltpu.SemaphoreType.DMA((80,)),
     ]
     vmem = pl.BlockSpec(memory_space=pltpu.VMEM)

time: 84.2 us -> 83.9 us (level)
  no operation moved by 1% of the time
where the time goes in v4:
time: 83.9 us; the launch traced here: 83.7 us
  Pallas kernels  80.4 us (96%)
  local copies, waits for them, and re-layouts  2.63 us (3%)
    pallas_call x1, Pallas kernels, shards(): pl.pallas_call(body, out_shape=jax.ShapeDtypeStruct((256 // N_TM, 1024),...  80.4 us
    unnamed x7, local copies, waits for them, and re-layouts  2.63 us

profile of v4, /device:TPU:1, one launch (start us, length us, event | category | flops | bytes accessed | tf_op | source)
XLA Modules:
  0.0 83.7 jit_solution(16914632932222322253)
XLA Ops:
  0.0 0.0 copy-start.2
  0.7 0.0 copy-done.2
  0.7 0.0 copy-start
  0.7 0.9 %copy-done = f32[1,64,1,8,128]{4,3,2,1,0:T(8,128)S(1)} copy-done((f32[1,64,1,8,128]{4,3,2,1,0:T(8,128)S(1)}, f32[1,64,1,8,128]{4,3,2,1,0:T(8,128)}, u32[]{:S(2)}) %copy-start) | copy-done | bytes 262168
  1.6 0.0 copy-start.1
  1.6 0.9 %copy-done.1 = f32[64,1,8,128]{3,2,1,0:T(8,128)S(1)} copy-done((f32[64,1,8,128]{3,2,1,0:T(8,128)S(1)}, f32[64,1,8,128]{3,2,1,0:T(8,128)}, u32[]{:S(2)}) %copy-start.1) | copy-done | bytes 262168
  2.6 80.4 %merge_tree.1 = f32[64,1024]{1,0:T(8,128)S(1)} custom-call(f32[512,128]{1,0:T(8,128)S(1)} %bitcast.3, f32[512,128]{1,0:T(8,128)S(1)} %bitcast.4, f32[8,128]{1,0:T(8,128)S(1)} %bitcast.5, s32[1]{0:T(128)S(6)} %copy.6.refs_3_), custom_call_target="tpu_custom_call" | custom-call | tf_op jit(solution)/shard_map/merge_tree/pallas_call | solution.py:478
  83.0 0.7 copy.7
Async XLA Ops:
  0.0 0.7 copy-start.2
  0.7 0.9 %copy-start = (f32[1,64,1,8,128]{4,3,2,1,0:T(8,128)S(1)}, f32[1,64,1,8,128]{4,3,2,1,0:T(8,128)}, u32[]{:S(2)}) copy-start(f32[1,64,1,8,128]{4,3,2,1,0:T(8,128)} %param.4) | copy-start | bytes 786436
  1.6 0.9 %copy-start.1 = (f32[64,1,8,128]{3,2,1,0:T(8,128)S(1)}, f32[64,1,8,128]{3,2,1,0:T(8,128)}, u32[]{:S(2)}) copy-start(f32[64,1,8,128]{3,2,1,0:T(8,128)} %param.5) | copy-start | bytes 786436

commit v5 on v4

--- a/solution.py
+++ b/solution.py
@@ -406,13 +406,8 @@
     send_h = links.group([(hb.at[core], hb.at[core], partner)], hb.at[core])
     send_w.wait()
 
-    merged = []
-    for p in range(2):
-        wh[...], wl[...] = split(wb[p])
-        terms = [dot3(wh[:, 256 * i:256 * i + 256], wl[:, 256 * i:256 * i + 256],
-                      sh[2 * p + i, :, pl.ds(0, 256)], sl[2 * p + i, :, pl.ds(0, 256)]) for i in range(2)]
-        merged.append(terms[0] + terms[1])
     send_c.wait()
+    wh[...], wl[...] = split(wb[1])
     for i in range(2):
         c_rows = jnp.concatenate([jnp.concatenate([cb[i, pl.ds(128 * n, 128)] for n in order], 1)
                                   for order in ((6, 0, 7, 3), (1, 2, 4, 5))], 0)
@@ -423,7 +418,10 @@
     send_h.wait()
     alphas = [hb[p, pl.ds(256, 1)] for p in range(2)]
     for p in range(2):
-        mh[halves[p]], ml[halves[p]] = split(merged[p] * alphas[p])
+        ah, al = split(wb[p])
+        terms = [dot3(ah[:, 256 * i:256 * i + 256], al[:, 256 * i:256 * i + 256],
+                      sh[2 * p + i, :, pl.ds(0, 256)], sl[2 * p + i, :, pl.ds(0, 256)]) for i in range(2)]
+        mh[halves[p]], ml[halves[p]] = split((terms[0] + terms[1]) * alphas[p])
     energy = weights(hb[0, pl.ds(0, 256)], cross * (alphas[0] * alphas[1]), hb[1, pl.ds(0, 256)],
                      jnp.sum(hb[0, pl.ds(264, 1), pl.ds(0, 1)] + hb[1, pl.ds(264, 1), pl.ds(0, 1)]))
     bs[...] = dot3(wh[...], wl[...], mh[...], ml[...])

time: 83.9 us -> 83.6 us (level)
  no operation moved by 1% of the time
where the time goes in v5:
time: 83.6 us; the launch traced here: 83.4 us
  Pallas kernels  80.1 us (96%)
  local copies, waits for them, and re-layouts  2.63 us (3%)
    pallas_call x1, Pallas kernels, shards(): pl.pallas_call(body, out_shape=jax.ShapeDtypeStruct((256 // N_TM, 1024),...  80.1 us
    unnamed x7, local copies, waits for them, and re-layouts  2.63 us

profile of v5, /device:TPU:1, one launch (start us, length us, event | category | flops | bytes accessed | tf_op | source)
XLA Modules:
  0.0 83.4 jit_solution(1120300337740292598)
XLA Ops:
  0.0 0.0 copy-start.2
  0.7 0.0 copy-done.2
  0.7 0.0 copy-start
  0.7 0.9 %copy-done = f32[1,64,1,8,128]{4,3,2,1,0:T(8,128)S(1)} copy-done((f32[1,64,1,8,128]{4,3,2,1,0:T(8,128)S(1)}, f32[1,64,1,8,128]{4,3,2,1,0:T(8,128)}, u32[]{:S(2)}) %copy-start) | copy-done | bytes 262168
  1.6 0.0 copy-start.1
  1.6 0.9 %copy-done.1 = f32[64,1,8,128]{3,2,1,0:T(8,128)S(1)} copy-done((f32[64,1,8,128]{3,2,1,0:T(8,128)S(1)}, f32[64,1,8,128]{3,2,1,0:T(8,128)}, u32[]{:S(2)}) %copy-start.1) | copy-done | bytes 262168
  2.6 80.1 %merge_tree.1 = f32[64,1024]{1,0:T(8,128)S(1)} custom-call(f32[512,128]{1,0:T(8,128)S(1)} %bitcast.3, f32[512,128]{1,0:T(8,128)S(1)} %bitcast.4, f32[8,128]{1,0:T(8,128)S(1)} %bitcast.5, s32[1]{0:T(128)S(6)} %copy.6.refs_3_), custom_call_target="tpu_custom_call" | custom-call | tf_op jit(solution)/shard_map/merge_tree/pallas_call | solution.py:476
  82.7 0.7 copy.7
Async XLA Ops:
  0.0 0.7 copy-start.2
  0.7 0.9 %copy-start = (f32[1,64,1,8,128]{4,3,2,1,0:T(8,128)S(1)}, f32[1,64,1,8,128]{4,3,2,1,0:T(8,128)}, u32[]{:S(2)}) copy-start(f32[1,64,1,8,128]{4,3,2,1,0:T(8,128)} %param.4) | copy-start | bytes 786436
  1.6 0.9 %copy-start.1 = (f32[64,1,8,128]{3,2,1,0:T(8,128)S(1)}, f32[64,1,8,128]{3,2,1,0:T(8,128)}, u32[]{:S(2)}) copy-start(f32[64,1,8,128]{3,2,1,0:T(8,128)} %param.5) | copy-start | bytes 786436
